TPU v7x, 512 devices: a whole 4x4x16 slice. The times are simulated.
512 devices in a mesh: row: 8 (over z_lo), col: 8 (over x, core), depth: 8 (over y, z_hi).
Axes of the slice: x: 4, y: 4, z: 16 (z_hi: 2, z_lo: 8; z = z_hi * 8 + z_lo), core: 2. Of those that a mesh axis runs over, the one named last changes fastest.
Arguments:
- query_rows: bfloat16 [8, 512, 6144], P('depth', 'col', 'row'), may hold values from -20 to 20
- key_rows: bfloat16 [8, 512, 6144], P('depth', 'col', 'row'), may hold values from -20 to 20
- value_rows: bfloat16 [8, 512, 6144], P('depth', 'col', 'row'), may hold values from -6 to 6
- positions: int32 [8, 512], P('depth'), may hold values from 0 to 511, as said below
- out_weight: bfloat16 [6144, 12288], P('row', 'col'), may hold values from -0.078125 to 0.078125
- out_grad: bfloat16 [8, 512, 12288], P('depth', 'row', 'col'), may hold values from -4 to 4
Outputs:
- layer_out: bfloat16 [8, 512, 12288], P('depth', 'row', 'col')
- query_grad: bfloat16 [8, 512, 6144], P('depth', 'col', 'row')
- key_grad: bfloat16 [8, 512, 6144], P('depth', 'col', 'row')
- value_grad: bfloat16 [8, 512, 6144], P('depth', 'col', 'row')
- weight_grad: float32 [6144, 12288], P('row', ('col', 'depth'))
Inputs may be any that keep to these rules, and one draw needn't show every extreme that they name: Each row is a permutation of 0 to 511. Cut a sequence into 16 blocks of consecutive positions; tokens 512 // 8 * c to 512 // 8 * (c + 1) - 1 hold the positions of block p and of block 15 - p for some p, in some order.
All inputs are finite; a program needn't handle non-finite values.
Results may differ from a plain program's by a relative error of at most 0.035.
Values may be sent and summed in bfloat16 or wider, within the bound.
A program may use at most 128 MiB of HBM per device.

v0:
```python
import jax
import jax.numpy as jnp
from jax import lax
from jax.sharding import PartitionSpec as P

HEAD_DIM = 128


def split_heads(tensor):
    return tensor.reshape(tensor.shape[0], tensor.shape[1], tensor.shape[2] // HEAD_DIM, HEAD_DIM)


def masked_logits(query_part, key_part, query_pos, key_pos):
    logits = jnp.einsum(
        "sqhd,skhd->shqk",
        split_heads(query_part),
        split_heads(key_part),
        preferred_element_type=jnp.float32,
    )
    logits = logits * HEAD_DIM ** (-0.5)
    visible = key_pos[:, None, None, :] <= query_pos[:, None, :, None]
    return jnp.where(visible, logits, -jnp.inf)


def softmax_stats(logits):
    highest = jnp.max(logits, axis=-1)
    denominator = jnp.sum(jnp.exp(logits - highest[..., None]), axis=-1)
    return (highest, denominator)


def head_inner(first_part, second_part):
    summed = jnp.sum(
        split_heads(first_part).astype(jnp.float32) * split_heads(second_part).astype(jnp.float32),
        axis=-1,
    )
    return jnp.transpose(summed, (0, 2, 1))


def local(query_rows, key_rows, value_rows, positions, out_weight, out_grad):
    seqs, span, width = query_rows.shape
    head_scale = HEAD_DIM ** (-0.5)
    own_pos = lax.dynamic_slice_in_dim(positions, lax.axis_index("col") * span, span, 1)
    key_all, value_all = (
        lax.all_gather(key_rows, "col", axis=1, tiled=True),
        lax.all_gather(value_rows, "col", axis=1, tiled=True),
    )
    logits = masked_logits(query_rows, key_all, own_pos, positions)
    highest, denominator = softmax_stats(logits)
    log_norm = highest + jnp.log(denominator)
    attn_probs = (jnp.exp(logits - highest[..., None]) / denominator[..., None]).astype(
        jnp.bfloat16
    )
    context = jnp.einsum(
        "shqk,skhd->sqhd", attn_probs, split_heads(value_all), preferred_element_type=jnp.float32
    )
    context = context.reshape(seqs, span, width).astype(jnp.bfloat16)
    context_all = lax.all_gather(context, "col", axis=1, tiled=True)
    window = context_all
    layer_out = lax.psum_scatter(
        jnp.einsum("slk,kn->lsn", window, out_weight, preferred_element_type=jnp.float32).astype(
            jnp.bfloat16
        ),
        "row",
        scatter_dimension=0,
        tiled=True,
    ).astype(jnp.float32)
    layer_out = jnp.transpose(layer_out, (1, 0, 2)).astype(jnp.bfloat16)
    grad_all = lax.all_gather(out_grad, "row", axis=1, tiled=True)
    window = grad_all
    context_grad = lax.psum_scatter(
        jnp.einsum("sln,kn->lsk", window, out_weight, preferred_element_type=jnp.float32).astype(
            jnp.bfloat16
        ),
        "col",
        scatter_dimension=0,
        tiled=True,
    ).astype(jnp.float32)
    context_grad = jnp.transpose(context_grad, (1, 0, 2)).astype(jnp.bfloat16)
    partial_grad = jnp.einsum(
        "slk,sln->kn", context_all, grad_all, preferred_element_type=jnp.float32
    )
    weight_grad = lax.psum_scatter(
        partial_grad.astype(jnp.bfloat16), "depth", scatter_dimension=1, tiled=True
    ).astype(jnp.float32)
    row_dot = head_inner(context_grad, context)
    weights = jnp.exp(logits - log_norm[..., None])
    dprob = jnp.einsum(
        "sqhd,skhd->shqk",
        split_heads(context_grad),
        split_heads(value_all),
        preferred_element_type=jnp.float32,
    )
    dlogits = (weights * (dprob - row_dot[..., None])).astype(jnp.bfloat16)
    query_grad = jnp.einsum(
        "shqk,skhd->sqhd", dlogits, split_heads(key_all), preferred_element_type=jnp.float32
    )
    query_grad = (head_scale * query_grad).reshape(seqs, span, width).astype(jnp.bfloat16)
    query_all, cgrad_all = (
        lax.all_gather(query_rows, "col", axis=1, tiled=True),
        lax.all_gather(context_grad, "col", axis=1, tiled=True),
    )
    norm_all, dot_all = (
        lax.all_gather(log_norm, "col", axis=2, tiled=True),
        lax.all_gather(row_dot, "col", axis=2, tiled=True),
    )
    key_logits = masked_logits(query_all, key_rows, positions, own_pos)
    key_weights = jnp.exp(key_logits - norm_all[..., None])
    key_dprob = jnp.einsum(
        "sqhd,skhd->shqk",
        split_heads(cgrad_all),
        split_heads(value_rows),
        preferred_element_type=jnp.float32,
    )
    key_dlogits = (key_weights * (key_dprob - dot_all[..., None])).astype(jnp.bfloat16)
    key_grad = jnp.einsum(
        "shqk,sqhd->skhd", key_dlogits, split_heads(query_all), preferred_element_type=jnp.float32
    )
    key_grad = (head_scale * key_grad).reshape(seqs, span, width).astype(jnp.bfloat16)
    value_grad = jnp.einsum(
        "shqk,sqhd->skhd",
        key_weights.astype(jnp.bfloat16),
        split_heads(cgrad_all),
        preferred_element_type=jnp.float32,
    )
    value_grad = value_grad.reshape(seqs, span, width).astype(jnp.bfloat16)
    return (layer_out, query_grad, key_grad, value_grad, weight_grad)


def solution(mesh):
    placed = (
        P("depth", "col", "row"),
        P("depth", "col", "row"),
        P("depth", "col", "row"),
        P("depth", None),
        P("row", "col"),
        P("depth", "row", "col"),
    )
    return jax.shard_map(
        local,
        mesh=mesh,
        in_specs=placed,
        out_specs=(
            P("depth", "row", "col"),
            P("depth", "col", "row"),
            P("depth", "col", "row"),
            P("depth", "col", "row"),
            P("row", ("col", "depth")),
        ),
        check_vma=False,
    )
```

profile of v0, /device:TPU:24, one launch (start us, length us, event | category | flops | bytes accessed | tf_op | source)
XLA Modules:
  0.0 368.2 jit_solution(17688467616718928089)
XLA Ops:
  7.2 0.0 copy-start
  7.2 0.0 all-gather.5.cloned.1.call-start
  7.2 0.7 all-gather.5.cloned.1.call-update
  7.9 0.0 reduce-scatter.10.cloned.1.call-start
  8.0 75.5 %all-gather.5.cloned.1.call-done = bf16[1,512,1536]{2,1,0:T(8,128)(2,1)} async-done(((bf16[1,64,1536]{2,1,0:T(8,128)(2,1)}), bf16[1,512,1536]{2,1,0:T(8,128)(2,1)}) %all-gather.5.cloned.1.call-update) | async-done | bytes 1572880 | tf_op jit(solution)/shard_map/all_gather | solution.py:68
  83.4 0.0 copy-done
  83.4 2.8 fusion.7
  86.3 0.0 copy-start.6
  86.3 0.0 copy-start.5
  86.3 1.2 copy.143
  87.4 0.0 reduce-scatter.10.cloned.1.call-update
  87.5 0.0 reduce-scatter.8.cloned.1.call-start
  87.5 0.0 copy-done.6
  87.5 0.0 copy-start.7
  87.5 0.0 copy-start.8
  87.6 13.9 %all_gather.25 = bf16[1,512,768]{2,1,0:T(8,128)(2,1)S(1)} all-gather(bf16[1,64,768]{2,1,0:T(8,128)(2,1)S(1)} %copy-done.6), channel_id=1, replica_groups=mesh['row'=8,'col'=8,'depth'=8] {'col'}, dimensions={1}, use_global_device_ids=true | all-gather | bytes 884736 | tf_op jit(solution)/shard_map/all_gather | solution.py:45
  101.4 1.2 copy.109
  102.6 0.0 copy-done.5
  102.6 15.0 %all_gather.24 = bf16[1,512,768]{2,1,0:T(8,128)(2,1)} all-gather(bf16[1,64,768]{2,1,0:T(8,128)(2,1)S(1)} %copy-done.5), channel_id=1, replica_groups=mesh['row'=8,'col'=8,'depth'=8] {'col'}, dimensions={1}, use_global_device_ids=true | all-gather | bytes 884736 | tf_op jit(solution)/shard_map/all_gather | solution.py:44
  117.6 1.4 copy.106
  119.0 0.0 copy-done.7
  119.0 0.0 copy-start.2
  119.0 0.1 reshape.351
  119.2 0.0 copy-done.8
  119.2 0.1 dynamic-slice_bitcast_fusion
  119.3 0.1 broadcast_compare_fusion.1
  119.4 0.3 fusion.43
  119.7 0.0 copy-start.3
  119.7 0.9 copy-done.3
  120.6 0.3 fusion.31
  120.9 1.5 reduce-scatter.10.cloned.1.call-done
  122.4 1.1 copy.144
  123.4 0.0 copy-done.9
  123.4 0.1 copy.114
  123.6 0.8 reshape.360
  124.4 2.1 fusion.38
  126.5 13.5 %all_gather.26 = bf16[1,512,768]{2,1,0:T(8,128)(2,1)S(1)} all-gather(bf16[1,64,768]{2,1,0:T(8,128)(2,1)S(1)} %copy_bitcast_fusion.3), channel_id=1, replica_groups=mesh['row'=8,'col'=8,'depth'=8] {'col'}, dimensions={1}, use_global_device_ids=true | all-gather | bytes 884736 | tf_op jit(solution)/shard_map/all_gather | solution.py:57
  140.0 2.9 convolution_convert_fusion
  142.9 0.0 reduce-scatter.8.cloned.1.call-update
  142.9 0.0 reduce-scatter.6.cloned.1.call-start
  142.9 2.5 fusion
  145.5 0.0 reduce-scatter.6.cloned.1.call-update
  145.5 0.8 reshape.357
  146.3 1.7 reshape.359
  148.0 14.7 %all_gather.28 = bf16[1,512,768]{2,1,0:T(8,128)(2,1)} all-gather(bf16[1,64,768]{2,1,0:T(8,128)(2,1)} %param.6), channel_id=1, replica_groups=mesh['row'=8,'col'=8,'depth'=8] {'col'}, dimensions={1}, use_global_device_ids=true | all-gather | bytes 884736 | tf_op jit(solution)/shard_map/all_gather | solution.py:99
  162.6 1.4 copy.118
  164.1 12.8 %all-gather.2 = f32[8,64,6]{1,2,0:T(8,128)S(1)} all-gather(f32[1,64,6]{1,2,0:T(8,128)S(1)} %bitcast.113), channel_id=2, replica_groups=mesh['row'=8,'col'=8,'depth'=8] {'col'}, dimensions={0}, use_global_device_ids=true | all-gather | bytes 13824 | tf_op jit(solution)/shard_map/all_gather | solution.py:103
  176.9 0.1 reshape.366
  177.0 0.8 broadcast_compare_fusion
  177.7 2.1 fusion.14
  179.9 2.2 fusion.25
  182.0 0.7 copy.165
  182.7 14.4 %all-gather.1 = bf16[512,1,768]{2,0,1:T(8,128)(2,1)} all-gather(bf16[64,1,768]{2,0,1:T(8,128)(2,1)S(1)} %copy.114), channel_id=3, replica_groups=mesh['row'=8,'col'=8,'depth'=8] {'col'}, dimensions={0}, use_global_device_ids=true | all-gather | bytes 884736 | tf_op jit(solution)/shard_map/all_gather | solution.py:100
  197.2 1.5 copy.123
  198.6 0.7 copy.126
  199.3 13.0 %all_gather.31 = f32[1,6,512]{1,0,2:T(1,128)S(1)} all-gather(f32[1,6,64]{1,0,2:T(1,128)} %copy.126), channel_id=1, replica_groups=mesh['row'=8,'col'=8,'depth'=8] {'col'}, dimensions={2}, use_global_device_ids=true | all-gather | bytes 13824 | tf_op jit(solution)/shard_map/all_gather | solution.py:104
  212.4 0.1 copy.127
  212.5 1.5 fusion.26
  214.0 0.0 copy-done.4
  214.0 1.8 fusion.24
  215.9 0.7 copy_bitcast_fusion
  216.6 80.4 %reduce-scatter.8.cloned.1.call-done = bf16[768,192]{0,1:T(8,128)(2,1)} async-done(((bf16[768,1536]{0,1:T(8,128)(2,1)}), bf16[768,192]{0,1:T(8,128)(2,1)}) %reduce-scatter.8.cloned.1.call-update) | async-done | bytes 294928 | tf_op jit(solution)/shard_map/reduce_scatter | solution.py:82
  296.9 1.8 convert_element_type.235
  298.7 62.9 %reduce-scatter.6.cloned.1.call-done = bf16[64,1,1536]{2,0,1:T(8,128)(2,1)} async-done(((bf16[512,1,1536]{2,0,1:T(8,128)(2,1)}), bf16[64,1,1536]{2,0,1:T(8,128)(2,1)}) %reduce-scatter.6.cloned.1.call-update) | async-done | bytes 196624 | tf_op jit(solution)/shard_map/reduce_scatter | solution.py:59
  (10 shorter events, 0.0 us)
Async XLA Ops:
  7.2 76.3 %copy-start = (bf16[768,1536]{1,0:T(8,128)(2,1)S(1)}, bf16[768,1536]{1,0:T(8,128)(2,1)}, u32[]{:S(2)}) copy-start(bf16[768,1536]{1,0:T(8,128)(2,1)} %param.10) | copy-start | bytes 7077892
  7.2 76.3 %all-gather.5.cloned.1.call-start = ((), (), s32[]{:S(2)}) async-start(), calls=%async_computation.4 | async-start | bytes 1769472 | tf_op jit(solution)/shard_map/all_gather | solution.py:68
  7.9 114.5 %reduce-scatter.10.cloned.1.call-start = ((), (), s32[]{:S(2)}) async-start(), calls=%async_computation.6 | async-start | bytes 884736
  86.3 1.3 copy-start.6
  86.3 16.3 %copy-start.5 = (bf16[1,64,768]{2,1,0:T(8,128)(2,1)S(1)}, bf16[1,64,768]{2,1,0:T(8,128)(2,1)}, u32[]{:S(2)}) copy-start(bf16[1,64,768]{2,1,0:T(8,128)(2,1)} %param.7) | copy-start | bytes 294916
  87.5 209.4 %reduce-scatter.8.cloned.1.call-start = ((), (), s32[]{:S(2)}) async-start(), calls=%async_computation.5 | async-start | bytes 2654208 | tf_op jit(solution)/shard_map/reduce_scatter | solution.py:82
  87.5 31.5 %copy-start.7 = (bf16[1,64,768]{2,1,0:T(8,128)(2,1)S(1)}, bf16[1,64,768]{2,1,0:T(8,128)(2,1)}, u32[]{:S(2)}) copy-start(bf16[1,64,768]{2,1,0:T(8,128)(2,1)} %param.6) | copy-start | bytes 294916
  87.5 31.6 %copy-start.8 = (s32[1,512]{1,0:T(1,128)S(1)}, s32[1,512]{1,0:T(1,128)}, u32[]{:S(2)}) copy-start(s32[1,512]{1,0:T(1,128)} %param.9) | copy-start | bytes 6148
  119.0 7.4 %copy-start.2 = (bf16[1,512,768]{1,2,0:T(8,128)(2,1)}, bf16[1,512,768]{1,2,0:T(8,128)(2,1)S(1)}, u32[]{:S(2)}) copy-start(bf16[1,512,768]{1,2,0:T(8,128)(2,1)S(1)} %copy.106) | copy-start | bytes 2359300
  119.3 4.2 %copy-start.9 = (s32[64]{0:T(128)}, s32[64]{0:T(128)S(1)}, u32[]{:S(2)}) copy-start(s32[64]{0:T(128)S(1)} %dynamic-slice_bitcast_fusion) | copy-start | bytes 772
  119.7 0.9 copy-start.3
  124.4 15.6 %copy-start.10 = (bf16[1,512,1536]{2,1,0:T(8,128)(2,1)S(1)}, bf16[1,512,1536]{2,1,0:T(8,128)(2,1)}, u32[]{:S(2)}) copy-start(bf16[1,512,1536]{2,1,0:T(8,128)(2,1)} %all-gather.5.cloned.1.call-done) | copy-start | bytes 4718596
  142.9 218.7 %reduce-scatter.6.cloned.1.call-start = ((), (), s32[]{:S(2)}) async-start(), calls=%async_computation.3 | async-start | bytes 1769472 | tf_op jit(solution)/shard_map/reduce_scatter | solution.py:59
  164.0 18.7 %copy-start.1 = (bf16[1,512,768]{1,2,0:T(8,128)(2,1)}, bf16[1,512,768]{1,2,0:T(8,128)(2,1)S(1)}, u32[]{:S(2)}) copy-start(bf16[1,512,768]{1,2,0:T(8,128)(2,1)S(1)} %copy.118) | copy-start | bytes 2359300
  197.2 16.8 %copy-start.4 = (bf16[64,6,128]{2,1,0:T(8,128)(2,1)S(1)}, bf16[64,6,128]{2,1,0:T(8,128)(2,1)}, u32[]{:S(2)}) copy-start(bf16[64,6,128]{2,1,0:T(8,128)(2,1)} %reshape.359) | copy-start | bytes 294916
Sparse Core Ops, SparseCore 0:
  10.1 73.2 all-gather.4
  87.6 34.7 reduce-scatter.9
  143.0 153.8 reduce-scatter.7
  300.2 61.3 reduce-scatter.5
where the time goes:
time: 369 us; the launch traced here: 368 us
  waiting for transfers between devices  221 us (60%)
  blocking collectives  97.3 us (26%)
  matrix products  18.3 us (5%)
  local copies, waits for them, and re-layouts  14.6 us (4%)
  between operations  14 us (4%)
    reduce_scatter x1, waiting for transfers between devices, local(): lax.psum_scatter(partial_grad.astype(jnp.bfloat16), 'depth', scatter_dime...  80.4 us
    all_gather x1, waiting for transfers between devices, local(): grad_all = lax.all_gather(out_grad, 'row', axis=1, tiled=True)  75.5 us
    reduce_scatter x1, waiting for transfers between devices, local(): lax.psum_scatter(jnp.einsum('slk,kn->lsn', window, out_weight, preferred_...  62.9 us
    all_gather x1, blocking collectives, local(): lax.all_gather(key_rows, 'col', axis=1, tiled=True)  15 us
    all_gather x1, blocking collectives, local(): lax.all_gather(query_rows, 'col', axis=1, tiled=True)  14.7 us
    all_gather x1, blocking collectives, local(): lax.all_gather(context_grad, 'col', axis=1, tiled=True)  14.4 us
    all_gather x1, blocking collectives, local(): lax.all_gather(value_rows, 'col', axis=1, tiled=True)  13.9 us
    all_gather x1, blocking collectives, local(): context_all = lax.all_gather(context, 'col', axis=1, tiled=True)  13.5 us
  transfers between devices with their start and end apart: 4, of which 4 were waited for; matrix products, arithmetic and copies ran while one was open for 6% of the time, Pallas kernels for 0%

commit v1 on v0

v1 whole, which is shorter than its diff:
```python
import functools

import jax
import jax.numpy as jnp
from jax import lax
from jax.experimental import pallas as pl
from jax.experimental.pallas import tpu as pltpu
from jax.sharding import PartitionSpec as P

HEAD_DIM = 128
HALVES = 2
SUBS = 2
MESH = pl.DeviceIdType.MESH
F32, BF16 = jnp.float32, jnp.bfloat16

NT = (((1,), (1,)), ((), ()))
TN = (((0,), (0,)), ((), ()))


def kernel(
    n_row, n_col, n_depth,
    q_ref, k_ref, v_ref, pos_ref, w_hbm, g_ref,
    out_ref, dq_ref, dk_ref, dv_ref, dw_ref,
    w_ref, qkv, pos_col, probs, probs_b, dlogits, ctx_own, ctx_all, grad_all,
    cg_stage, cg_recv, cg_own, dqkv_own, dqkv_all,
    lo, rs_stage_r, rs_stage_l, rs_r, rs_l, dw_full, dw_sum, dw_stage, dw_recv,
    w_sem, qkv_ss, qkv_rs, ag_ss, ag_rs, ctx_ss, ctx_rs, cg_ss, cg_rs, dq_ss, dq_rs,
    rs_ss, rs_rs, dw_ss, dw_rs,
):
    r, c, d = lax.axis_index("row"), lax.axis_index("col"), lax.axis_index("depth")
    y, b = lax.div(d, HALVES), lax.rem(d, HALVES)
    ring, n_y = HALVES * n_row, n_depth // HALVES
    reach = n_row // 2
    z = b * n_row + r
    span, width = q_ref.shape[1:]
    rows, cols = g_ref.shape[1:]
    length = pos_ref.shape[1]
    heads = width // HEAD_DIM
    scale = HEAD_DIM ** (-0.5)

    def on_ring(place):
        place = lax.rem(place + 2 * ring, ring)
        return {"row": lax.rem(place, n_row), "depth": y * HALVES + lax.div(place, n_row)}

    def on_y(place):
        return {"depth": lax.rem(place + n_y, n_y) * HALVES + b}

    def chunk_at(offset):
        return lax.rem(z + offset + 2 * ring, ring)

    def owner(h):
        return (h * n_col) // heads

    right, left, up, down = on_ring(z + 1), on_ring(z - 1), on_y(y + 1), on_y(y - 1)
    other = {"depth": y * HALVES + 1 - b}
    head, is_head = 0, c == owner(0)
    for h in range(1, heads):
        head = jnp.where(c >= owner(h), h, head)
        is_head = jnp.logical_or(is_head, c == owner(h))
    head_cols = pl.ds(pl.multiple_of(head * HEAD_DIM, HEAD_DIM), HEAD_DIM)
    fixed_cols = [pl.ds(h * HEAD_DIM, HEAD_DIM) for h in range(heads)]
    sub_cols = [pl.ds(u * (cols // SUBS), cols // SUBS) for u in range(SUBS)]

    def send(src, dst, send_sem, recv_sem, to):
        return pltpu.make_async_remote_copy(
            src_ref=src, dst_ref=dst, send_sem=send_sem, recv_sem=recv_sem,
            device_id=to, device_id_type=MESH,
        )

    def wait_bytes(ref, sem):
        pltpu.make_async_copy(ref, ref, sem).wait()

    barrier = pltpu.get_barrier_semaphore()
    peers = [{"col": lax.rem(c + i, n_col)} for i in range(1, n_col)]
    peers += [right, left, other, up]
    if n_y > 2:
        peers += [down]
    for peer in peers:
        pl.semaphore_signal(barrier, inc=1, device_id=peer, device_id_type=MESH)
    weight_copy = pltpu.make_async_copy(w_hbm, w_ref, w_sem)
    weight_copy.start()
    grad_all[z] = g_ref[0]
    pl.semaphore_wait(barrier, len(peers))

    drain = []

    far = [ring // 2, ring // 2 - 1]

    def grad_copy(way, step, u):
        held = chunk_at((1 - step) if way == 0 else (step - 1))
        block = grad_all.at[held, :, sub_cols[u]]
        return send(block, block, ag_ss.at[way, step - 1, u], ag_rs.at[way, step - 1, u],
                    right if way == 0 else left)

    def grad_arrives(way, step, u):
        block = grad_all.at[chunk_at(-step if way == 0 else step), :, sub_cols[u]]
        send(block, block, ag_ss.at[way, step - 1, u], ag_rs.at[way, step - 1, u], right).wait_recv()

    def grad_start(way, step, u):
        copy = grad_copy(way, step, u)
        copy.start()
        drain.append(copy.wait_send)

    def grad_step(step):
        for u in range(SUBS):
            for way in range(2):
                if step <= far[way]:
                    grad_arrives(way, step, u)
                    if step < far[way]:
                        grad_start(way, step + 1, u)

    for u in range(SUBS):
        for way in range(2):
            grad_start(way, 1, u)

    for h in range(heads):
        for t, ref in enumerate((q_ref, k_ref, v_ref)):
            place = pl.ds(pl.multiple_of(c * span, span), span)

            def copy_of(h=h, t=t, ref=ref, place=place):
                return send(ref.at[0, :, fixed_cols[h]], qkv.at[t, place, :],
                            qkv_ss.at[t, h], qkv_rs.at[t, c], {"col": owner(h)})

            @pl.when(c != owner(h))
            def _(copy_of=copy_of):
                copy_of().start()

            @pl.when(c == owner(h))
            def _(h=h, t=t, ref=ref, place=place):
                qkv[t, place, :] = ref[0, :, fixed_cols[h]]

            def wait_sent(h=h, copy_of=copy_of):
                @pl.when(c != owner(h))
                def _():
                    copy_of().wait_send()

            drain.append(wait_sent)

    block_rows = min(128, length)

    def forward(first, last):
        @pl.when(is_head)
        def _():
            @pl.loop(first, last)
            def _(i):
                at = pl.ds(pl.multiple_of(i * block_rows, block_rows), block_rows)
                logits = lax.dot_general(qkv[0, at, :], qkv[1], NT, preferred_element_type=F32)
                visible = pos_ref[...].astype(F32) <= pos_col[at, 0:1]
                logits = jnp.where(visible, logits * scale, -jnp.inf)
                highest = jnp.max(logits, axis=-1, keepdims=True)
                grown = jnp.exp(logits - highest)
                prob = grown / jnp.sum(grown, axis=-1, keepdims=True)
                probs[at, :] = prob
                rounded = prob.astype(BF16)
                probs_b[at, :] = rounded
                context = jnp.dot(rounded, qkv[2], preferred_element_type=F32)
                ctx_own[at, :] = context.astype(BF16)

    n_blocks = length // block_rows
    grad_step(1)

    @pl.when(is_head)
    def _():
        pos_col[...] = jnp.transpose(
            jnp.broadcast_to(pos_ref[...].astype(F32), (128, length))
        )
        for i in range(1, n_col):
            src = lax.rem(c + i, n_col)
            for t in range(3):
                place = qkv.at[t, pl.ds(pl.multiple_of(src * span, span), span), :]
                send(place, place, qkv_ss.at[t, 0], qkv_rs.at[t, src], {"col": src}).wait_recv()

    forward(0, n_blocks // 2)
    grad_step(2)
    forward(n_blocks // 2, n_blocks)

    def ctx_copy(half, i):
        if half == 0:
            src, place = ctx_own, b
        else:
            place = 1 - b
            src = ctx_all.at[pl.ds(pl.multiple_of(place * length, length), length), head_cols]
        dst = ctx_all.at[pl.ds(pl.multiple_of(place * length, length), length), head_cols]
        return send(src, dst, ctx_ss.at[half, i], ctx_rs.at[half, head], {"col": lax.rem(c + i, n_col)})

    def ctx_cross():
        dst = ctx_all.at[pl.ds(pl.multiple_of(b * length, length), length), head_cols]
        return send(ctx_own, dst, ctx_ss.at[0, 0], ctx_rs.at[1, head], other)

    def ctx_arrives(half, h, place_cols):
        place = b if half == 0 else 1 - b
        dst = ctx_all.at[pl.ds(pl.multiple_of(place * length, length), length), place_cols]
        send(dst, dst, ctx_ss.at[0, 0], ctx_rs.at[half, h], other).wait_recv()

    @pl.when(is_head)
    def _():
        ctx_cross().start()
        for i in range(1, n_col):
            ctx_copy(0, i).start()
        ctx_all[pl.ds(pl.multiple_of(b * length, length), length), head_cols] = ctx_own[...]

    def ctx_relay():
        @pl.when(is_head)
        def _():
            ctx_arrives(1, head, head_cols)
            for i in range(1, n_col):
                ctx_copy(1, i).start()

    def ctx_wait(half):
        for h in range(heads):
            @pl.when(c != owner(h))
            def _(h=h):
                ctx_arrives(half, h, fixed_cols[h])

    def ctx_drain():
        @pl.when(is_head)
        def _():
            ctx_cross().wait_send()
            for half in range(2):
                for i in range(1, n_col):
                    ctx_copy(half, i).wait_send()

    drain.append(ctx_drain)

    def context_grad(offset):
        block = r + offset

        @pl.when(jnp.logical_and(block >= 0, block < n_row))
        def _():
            held = chunk_at(offset)
            place = pl.ds(pl.multiple_of(block * rows, rows), rows)

            @pl.loop(0, heads // 2)
            def _(i):
                two = pl.ds(pl.multiple_of(i * 2 * HEAD_DIM, 2 * HEAD_DIM), 2 * HEAD_DIM)
                product = lax.dot_general(grad_all[held], w_ref[two, :], NT, preferred_element_type=F32)
                cg_stage[place, two] = product.astype(BF16)
                for k in range(2):
                    h = 2 * i + k
                    to = lax.div(h * n_col, heads)
                    own = pl.ds(pl.multiple_of(h * HEAD_DIM, HEAD_DIM), HEAD_DIM)

                    @pl.when(c != to)
                    def _(h=h, to=to, own=own):
                        send(cg_stage.at[place, own], cg_recv.at[c, place, :], cg_ss.at[h], cg_rs.at[c], {"col": to}).start()

                    @pl.when(c == to)
                    def _(k=k):
                        cg_recv[c, place, :] = product[:, k * HEAD_DIM:(k + 1) * HEAD_DIM].astype(BF16)

    def context_grads(first, last):
        if first == 0:
            context_grad(0)
        for step in range(max(first, 1), min(last, n_row - 1) + 1):
            @pl.loop(0, 2)
            def _(way, step=step):
                context_grad((2 * way - 1) * step)

    def cg_drain():
        for h in range(heads):
            @pl.when(c != owner(h))
            def _(h=h):
                wait_bytes(cg_recv.at[0], cg_ss.at[h])

    drain.append(cg_drain)

    tile = cols // 3

    def project(place):
        held = chunk_at(place - reach)
        tokens = ctx_all[pl.ds(pl.multiple_of(held * rows, rows), rows), :]

        @pl.loop(0, 3)
        def _(i):
            at = pl.ds(pl.multiple_of(i * tile, tile), tile)
            lo[place, :, at] = jnp.dot(tokens, w_ref[:, at], preferred_element_type=F32)

    def out_step(way, step, final=False):
        stage, landed = (rs_stage_r, rs_r) if way == 0 else (rs_stage_l, rs_l)
        place = (2 * reach - step) if way == 0 else step - 1
        for u in range(SUBS):
            total = lo[place, :, sub_cols[u]]
            if step > 1:
                block = landed.at[step - 2, :, sub_cols[u]]
                send(block, block, rs_ss.at[way, step - 2, u], rs_rs.at[way, step - 2, u], right).wait_recv()
                total = total + block[...].astype(F32)
            if final:
                lo[place, :, sub_cols[u]] = total
                continue
            stage[step - 1, :, sub_cols[u]] = total.astype(BF16)
            copy = send(stage.at[step - 1, :, sub_cols[u]], landed.at[step - 1, :, sub_cols[u]],
                        rs_ss.at[way, step - 1, u], rs_rs.at[way, step - 1, u], right if way == 0 else left)
            copy.start()
            drain.append(copy.wait_send)

    def out_both(step):
        if step < reach:
            project(2 * reach - step)
            out_step(0, step)
        if step <= reach:
            project(step - 1)
            out_step(1, step)

    stripe = cols // n_depth
    part = stripe // 2

    def weight_product(place):
        place = lax.rem(place + 2 * n_y, n_y)
        at = pl.ds(pl.multiple_of(place * 2 * stripe + b * 128, 128), 256)
        tokens = grad_all[:, :, at].reshape(ring * rows, 256)
        dw_full[...] = lax.dot_general(tokens, ctx_all[...], TN, preferred_element_type=F32)
        dw_sum[place] = dw_full[pl.ds(pl.multiple_of(b * 64, 64), stripe), :]

    def weight_step(way, step, final=False):
        place = lax.rem(y + (-step if way == 0 else step) + 2 * n_y, n_y)
        own = slice(way * part, (way + 1) * part)
        total = dw_sum[place, own, :]
        if step > 1:
            block = dw_recv.at[way, step - 2]
            send(block, block, dw_ss.at[way, step - 2], dw_rs.at[way, step - 2], up).wait_recv()
            total = total + block[...].astype(F32)
        if final:
            dw_ref[own, :] = total
            return
        dw_stage[way, step - 1] = total.astype(BF16)
        copy = send(dw_stage.at[way, step - 1], dw_recv.at[way, step - 1], dw_ss.at[way, step - 1],
                    dw_rs.at[way, step - 1], up if way == 0 else down)
        copy.start()
        drain.append(copy.wait_send)

    def backward():
        @pl.when(is_head)
        def _():
            for i in range(1, n_col):
                src = lax.rem(c + i, n_col)
                wait_bytes(cg_recv.at[src], cg_rs.at[src])

            @pl.loop(0, n_blocks)
            def _(i):
                at = pl.ds(pl.multiple_of(i * block_rows, block_rows), block_rows)
                total = cg_recv[0, at, :].astype(F32)
                for k in range(1, n_col):
                    total = total + cg_recv[k, at, :].astype(F32)
                grad = total.astype(BF16)
                cg_own[at, :] = grad
                row_dot = jnp.sum(grad.astype(F32) * ctx_own[at, :].astype(F32), axis=-1, keepdims=True)
                dprob = lax.dot_general(grad, qkv[2], NT, preferred_element_type=F32)
                rounded = (probs[at, :] * (dprob - row_dot)).astype(BF16)
                dlogits[at, :] = rounded
                query_grad = jnp.dot(rounded, qkv[1], preferred_element_type=F32) * scale
                dqkv_own[0, at, :] = query_grad.astype(BF16)

            key_grad = lax.dot_general(dlogits[...], qkv[0], TN, preferred_element_type=F32) * scale
            dqkv_own[1] = key_grad.astype(BF16)
            value_grad = lax.dot_general(probs_b[...], cg_own[...], TN, preferred_element_type=F32)
            dqkv_own[2] = value_grad.astype(BF16)
            for t in range(3):
                for i in range(1, n_col):
                    dqkv_copy(t, i).start()
                dqkv_all[t, :, head_cols] = dqkv_own[t, pl.ds(pl.multiple_of(c * span, span), span), :]

    def dqkv_copy(t, i):
        to = lax.rem(c + i, n_col)
        return send(dqkv_own.at[t, pl.ds(pl.multiple_of(to * span, span), span), :],
                    dqkv_all.at[t, :, head_cols], dq_ss.at[t, i], dq_rs.at[t, head], {"col": to})

    def dqkv_drain():
        @pl.when(is_head)
        def _():
            for t in range(3):
                for i in range(1, n_col):
                    dqkv_copy(t, i).wait_send()

    drain.append(dqkv_drain)

    last = ring // 2
    weight_copy.wait()
    context_grads(0, 1)
    grad_step(3) if last >= 3 else None
    context_grads(2, 3)
    grad_step(4) if last >= 4 else None
    ctx_relay()
    context_grads(4, 4)
    grad_step(5) if last >= 5 else None
    ctx_wait(0)
    ctx_wait(1)
    out_both(1)
    grad_step(6) if last >= 6 else None
    context_grads(5, 6)
    out_both(2)
    grad_step(7) if last >= 7 else None
    context_grads(7, n_row)
    out_both(3)
    for step in range(8, last + 1):
        grad_step(step)
    for step in range(4, reach + 1):
        out_both(step)
    project(reach)
    for offset in (-1, 1):
        weight_product(y + offset)
        weight_step(0 if offset < 0 else 1, 1)
    for offset in range(2, n_y - 1):
        weight_product(y + offset)
    weight_product(y)
    backward()
    for step in range(2, n_y):
        weight_step(0, step)
        weight_step(1, step)
    out_step(0, reach, final=True)
    out_step(1, reach + 1, final=True)
    out_ref[0] = lo[reach].astype(BF16)
    weight_step(0, n_y, final=True)
    weight_step(1, n_y, final=True)
    for t, ref in enumerate((dq_ref, dk_ref, dv_ref)):
        for h in range(heads):
            @pl.when(c != owner(h))
            def _(t=t, h=h):
                block = dqkv_all.at[t, :, fixed_cols[h]]
                send(block, block, dq_ss.at[t, 0], dq_rs.at[t, h], other).wait_recv()
        ref[0] = dqkv_all[t]
    for wait in drain:
        wait()


def solution(mesh):
    n_row, n_col, n_depth = mesh.shape["row"], mesh.shape["col"], mesh.shape["depth"]

    def local(q, k, v, positions, weight, grad):
        _, span, width = q.shape
        _, rows, cols = grad.shape
        length = positions.shape[1]
        heads, ring, reach, n_y = width // HEAD_DIM, HALVES * n_row, n_row // 2, n_depth // HALVES
        stripe = cols // n_depth
        vmem = pl.BlockSpec(memory_space=pltpu.VMEM)
        dma = pltpu.SemaphoreType.DMA
        hops, turns = max(reach, 1), max(n_y - 1, 1)
        scratch = [
            pltpu.VMEM((width, cols), BF16),
            pltpu.VMEM((3, length, HEAD_DIM), BF16),
            pltpu.VMEM((length, 128), F32),
            pltpu.VMEM((length, length), F32),
            pltpu.VMEM((length, length), BF16),
            pltpu.VMEM((length, length), BF16),
            pltpu.VMEM((length, HEAD_DIM), BF16),
            pltpu.VMEM((HALVES * length, width), BF16),
            pltpu.VMEM((ring, rows, cols), BF16),
            pltpu.VMEM((length, width), BF16),
            pltpu.VMEM((n_col, length, HEAD_DIM), BF16),
            pltpu.VMEM((length, HEAD_DIM), BF16),
            pltpu.VMEM((3, length, HEAD_DIM), BF16),
            pltpu.VMEM((3, span, width), BF16),
            pltpu.VMEM((2 * reach, rows, cols), F32),
            pltpu.VMEM((hops, rows, cols), BF16),
            pltpu.VMEM((hops, rows, cols), BF16),
            pltpu.VMEM((hops, rows, cols), BF16),
            pltpu.VMEM((hops, rows, cols), BF16),
            pltpu.VMEM((256, width), F32),
            pltpu.VMEM((n_y, stripe, width), F32),
            pltpu.VMEM((2, turns, stripe // 2, width), BF16),
            pltpu.VMEM((2, turns, stripe // 2, width), BF16),
            dma,
            dma((3, heads)), dma((3, n_col)),
            dma((2, ring // 2, SUBS)), dma((2, ring // 2, SUBS)),
            dma((2, n_col)), dma((2, heads)),
            dma((heads,)), dma((n_col,)),
            dma((3, n_col)), dma((3, heads)),
            dma((2, hops, SUBS)), dma((2, hops, SUBS)),
            dma((2, turns)), dma((2, turns)),
        ]
        layer_out, query_grad, key_grad, value_grad, weight_grad = pl.pallas_call(
            functools.partial(kernel, n_row, n_col, n_depth),
            out_shape=(
                jax.ShapeDtypeStruct(grad.shape, BF16),
                jax.ShapeDtypeStruct(q.shape, BF16),
                jax.ShapeDtypeStruct(k.shape, BF16),
                jax.ShapeDtypeStruct(v.shape, BF16),
                jax.ShapeDtypeStruct((stripe, width), F32),
            ),
            in_specs=[vmem] * 4 + [pl.BlockSpec(memory_space=pl.ANY), vmem],
            out_specs=(vmem,) * 5,
            scratch_shapes=scratch,
            compiler_params=pltpu.CompilerParams(
                collective_id=0, has_side_effects=True, vmem_limit_bytes=56 * 1024 * 1024
            ),
        )(q, k, v, positions, weight, grad)
        return layer_out, query_grad, key_grad, value_grad, weight_grad.T

    return jax.shard_map(
        local,
        mesh=mesh,
        in_specs=(
            P("depth", "col", "row"),
            P("depth", "col", "row"),
            P("depth", "col", "row"),
            P("depth", None),
            P("row", "col"),
            P("depth", "row", "col"),
        ),
        out_specs=(
            P("depth", "row", "col"),
            P("depth", "col", "row"),
            P("depth", "col", "row"),
            P("depth", "col", "row"),
            P("row", ("col", "depth")),
        ),
        check_vma=False,
    )
```

time: 369 us -> 111 us (0.30)
  waiting for transfers between devices: 221 us -> 0 us
  Pallas kernels: 0 us -> 101 us
  blocking collectives: 97.3 us -> 0 us
  matrix products: 18.3 us -> 0 us
  between operations: 14 us -> 0.64 us
  local copies, waits for them, and re-layouts: 14.6 us -> 8.15 us
    reduce_scatter x2 -> x0, waiting for transfers between devices: 143 us -> none  [the longest x1 80.4 us: local(): lax.psum_scatter(partial_grad.astype(jnp.bfloat16), 'depth', scatter_dime...]
    pallas_call x0 -> x1, Pallas kernels: none -> 101 us  [local(): pl.pallas_call(functools.partial(kernel, n_row, n_col, n_depth), out_shap...]
    all_gather x7 -> x0, blocking collectives: 97.3 us -> none  [the longest x1 15 us: local(): lax.all_gather(key_rows, 'col', axis=1, tiled=True)]
    all_gather x1 -> x0, waiting for transfers between devices: 75.5 us -> none  [local(): grad_all = lax.all_gather(out_grad, 'row', axis=1, tiled=True)]
    dot_general x9 -> x0, matrix products: 18.3 us -> none  [the longest x1 2.89 us: local(): jnp.einsum('slk,sln->kn', context_all, grad_all, preferred_element_type=j...]
    all_gather x5 -> x0, local copies, waits for them, and re-layouts: 5.48 us -> none  [the longest x1 1.46 us: local(): lax.all_gather(context_grad, 'col', axis=1, tiled=True)]
    unnamed x25 -> x5, local copies, waits for them, and re-layouts: 3.27 us -> 8.15 us
  transfers between devices with their start and end apart: 4 -> 0, of which waited for: 4 -> 0; matrix products, arithmetic and copies ran while one was open for 6% -> 0% of each run, Pallas kernels for 0% -> 0%
where the time goes in v1:
time: 111 us; the launch traced here: 110 us
  Pallas kernels  101 us (91%)
  local copies, waits for them, and re-layouts  8.15 us (7%)
    pallas_call x1, Pallas kernels, local(): pl.pallas_call(functools.partial(kernel, n_row, n_col, n_depth), out_shap...  101 us
    unnamed x5, local copies, waits for them, and re-layouts  8.15 us

profile of v1, /device:TPU:24, one launch (start us, length us, event | category | flops | bytes accessed | tf_op | source)
XLA Modules:
  0.0 110.0 jit_solution(853793153263795321)
XLA Ops:
  0.6 101.2 %shard_map.101 = (bf16[1,64,1536]{2,1,0:T(8,128)(2,1)}, bf16[1,64,768]{2,1,0:T(8,128)(2,1)}, bf16[1,64,768]{2,1,0:T(8,128)(2,1)}, bf16[1,64,768]{2,1,0:T(8,128)(2,1)}, f32[192,768]{1,0:T(8,128)}) custom-call(bf16[1,64,768]{2,1,0:T(8,128)(2,1)} %q_ref.1, bf16[1,64,768]{2,1,0:T(8,128)(2,1)} %k_ref.1, bf16[1,64,768]{2,1,0:T(8,128)(2,1)} %v_ref.1, ...), custom_call_target="tpu_custom_call" | custom-call | tf_op jit(solution)/shard_map/pallas_call | solution.py:470
  101.8 1.6 %copy.16 = bf16[1,64,1536]{2,1,0:T(8,128)(2,1)} copy(bf16[1,64,1536]{2,1,0:T(8,128)(2,1)} %get-tuple-element.20) | data formatting | bytes 393216
  103.5 1.5 %copy.17 = bf16[1,64,768]{2,1,0:T(8,128)(2,1)} copy(bf16[1,64,768]{2,1,0:T(8,128)(2,1)} %get-tuple-element.21) | data formatting | bytes 196608
  105.0 1.5 %copy.18 = bf16[1,64,768]{2,1,0:T(8,128)(2,1)} copy(bf16[1,64,768]{2,1,0:T(8,128)(2,1)} %get-tuple-element.22) | data formatting | bytes 196608
  106.5 1.5 %copy.19 = bf16[1,64,768]{2,1,0:T(8,128)(2,1)} copy(bf16[1,64,768]{2,1,0:T(8,128)(2,1)} %get-tuple-element.23) | data formatting | bytes 196608
  108.1 1.9 %copy.20 = f32[768,192]{0,1:T(8,128)} copy(f32[768,192]{0,1:T(8,128)} %bitcast.1) | data formatting | bytes 1179648

commit v2 on v1

--- a/solution.py
+++ b/solution.py
@@ -10,6 +10,7 @@
 HEAD_DIM = 128
 HALVES = 2
 SUBS = 2
+VMEM_BYTES = 56 * 1024 * 1024
 MESH = pl.DeviceIdType.MESH
 F32, BF16 = jnp.float32, jnp.bfloat16
 
@@ -21,10 +22,10 @@
     n_row, n_col, n_depth,
     q_ref, k_ref, v_ref, pos_ref, w_hbm, g_ref,
     out_ref, dq_ref, dk_ref, dv_ref, dw_ref,
-    w_ref, qkv, pos_col, probs, probs_b, dlogits, ctx_own, ctx_all, grad_all,
+    w_ref, qkv, pos_col, probs, probs_b, dlogits, ctx_own, ctx_all, ctx_rel, relay, grad_all,
     cg_stage, cg_recv, cg_own, dqkv_own, dqkv_all,
-    lo, rs_stage_r, rs_stage_l, rs_r, rs_l, dw_full, dw_sum, dw_stage, dw_recv,
-    w_sem, qkv_ss, qkv_rs, ag_ss, ag_rs, ctx_ss, ctx_rs, cg_ss, cg_rs, dq_ss, dq_rs,
+    lo, rs_stage_r, rs_stage_l, rs_r, rs_l, dw_sum, dw_stage, dw_recv,
+    w_sem, qkv_ss, qkv_rs, ag_ss, ag_rs, ctx_ss, ctx_rs, fwd_ss, cross_ss, cross_rs, cg_ss, cg_rs, dq_ss, dq_rs,
     rs_ss, rs_rs, dw_ss, dw_rs,
 ):
     r, c, d = lax.axis_index("row"), lax.axis_index("col"), lax.axis_index("depth")
@@ -46,13 +47,17 @@
         return {"depth": lax.rem(place + n_y, n_y) * HALVES + b}
 
     def chunk_at(offset):
-        return lax.rem(z + offset + 2 * ring, ring)
+        return lax.rem(z + turn * offset + 2 * ring, ring)
 
     def owner(h):
         return (h * n_col) // heads
 
-    right, left, up, down = on_ring(z + 1), on_ring(z - 1), on_y(y + 1), on_y(y - 1)
-    other = {"depth": y * HALVES + 1 - b}
+    core = lax.rem(c, 2)
+    turn = 1 - 2 * core
+    right, left, up, down = on_ring(z + turn), on_ring(z - turn), on_y(y + 1), on_y(y - 1)
+    sibling = {"col": c + 1 - 2 * core}
+    far_right, far_left = on_ring(z + turn * (n_row - 1)), on_ring(z - turn * (n_row - 1))
+    middle = ring // 2
     head, is_head = 0, c == owner(0)
     for h in range(1, heads):
         head = jnp.where(c >= owner(h), h, head)
@@ -72,14 +77,16 @@
 
     barrier = pltpu.get_barrier_semaphore()
     peers = [{"col": lax.rem(c + i, n_col)} for i in range(1, n_col)]
-    peers += [right, left, other, up]
+    peers += [right, left, up]
     if n_y > 2:
         peers += [down]
+    if n_row > 2:
+        peers += [far_right, far_left]
     for peer in peers:
         pl.semaphore_signal(barrier, inc=1, device_id=peer, device_id_type=MESH)
     weight_copy = pltpu.make_async_copy(w_hbm, w_ref, w_sem)
     weight_copy.start()
-    grad_all[z] = g_ref[0]
+    grad_all[middle] = g_ref[0]
     pl.semaphore_wait(barrier, len(peers))
 
     drain = []
@@ -87,14 +94,13 @@
     far = [ring // 2, ring // 2 - 1]
 
     def grad_copy(way, step, u):
-        held = chunk_at((1 - step) if way == 0 else (step - 1))
-        block = grad_all.at[held, :, sub_cols[u]]
-        return send(block, block, ag_ss.at[way, step - 1, u], ag_rs.at[way, step - 1, u],
-                    right if way == 0 else left)
+        sign = -1 if way == 0 else 1
+        return send(grad_all.at[middle + sign * (step - 1), :, sub_cols[u]],
+                    grad_all.at[middle + sign * step, :, sub_cols[u]],
+                    ag_ss.at[way, step - 1, u], ag_rs.at[way, step - 1, u], right if way == 0 else left)
 
     def grad_arrives(way, step, u):
-        block = grad_all.at[chunk_at(-step if way == 0 else step), :, sub_cols[u]]
-        send(block, block, ag_ss.at[way, step - 1, u], ag_rs.at[way, step - 1, u], right).wait_recv()
+        grad_copy(way, step, u).wait_recv()
 
     def grad_start(way, step, u):
         copy = grad_copy(way, step, u)
@@ -157,77 +163,124 @@
                 ctx_own[at, :] = context.astype(BF16)
 
     n_blocks = length // block_rows
-    grad_step(1)
-
-    @pl.when(is_head)
-    def _():
-        pos_col[...] = jnp.transpose(
-            jnp.broadcast_to(pos_ref[...].astype(F32), (128, length))
-        )
-        for i in range(1, n_col):
-            src = lax.rem(c + i, n_col)
-            for t in range(3):
-                place = qkv.at[t, pl.ds(pl.multiple_of(src * span, span), span), :]
-                send(place, place, qkv_ss.at[t, 0], qkv_rs.at[t, src], {"col": src}).wait_recv()
-
-    forward(0, n_blocks // 2)
-    grad_step(2)
-    forward(n_blocks // 2, n_blocks)
-
-    def ctx_copy(half, i):
-        if half == 0:
-            src, place = ctx_own, b
-        else:
-            place = 1 - b
-            src = ctx_all.at[pl.ds(pl.multiple_of(place * length, length), length), head_cols]
-        dst = ctx_all.at[pl.ds(pl.multiple_of(place * length, length), length), head_cols]
-        return send(src, dst, ctx_ss.at[half, i], ctx_rs.at[half, head], {"col": lax.rem(c + i, n_col)})
-
-    def ctx_cross():
-        dst = ctx_all.at[pl.ds(pl.multiple_of(b * length, length), length), head_cols]
-        return send(ctx_own, dst, ctx_ss.at[0, 0], ctx_rs.at[1, head], other)
-
-    def ctx_arrives(half, h, place_cols):
+
+    def heads_arrive():
+        @pl.when(is_head)
+        def _():
+            pos_col[...] = jnp.transpose(
+                jnp.broadcast_to(pos_ref[...].astype(F32), (128, length))
+            )
+            for i in range(1, n_col):
+                src = lax.rem(c + i, n_col)
+                for t in range(3):
+                    place = qkv.at[t, pl.ds(pl.multiple_of(src * span, span), span), :]
+                    send(place, place, qkv_ss.at[t, 0], qkv_rs.at[t, src], {"col": src}).wait_recv()
+
+    half_rows = length // 2
+
+    def ctx_rows(half):
         place = b if half == 0 else 1 - b
-        dst = ctx_all.at[pl.ds(pl.multiple_of(place * length, length), length), place_cols]
-        send(dst, dst, ctx_ss.at[0, 0], ctx_rs.at[half, h], other).wait_recv()
-
-    @pl.when(is_head)
-    def _():
-        ctx_cross().start()
-        for i in range(1, n_col):
-            ctx_copy(0, i).start()
-        ctx_all[pl.ds(pl.multiple_of(b * length, length), length), head_cols] = ctx_own[...]
-
-    def ctx_relay():
-        @pl.when(is_head)
-        def _():
-            ctx_arrives(1, head, head_cols)
-            for i in range(1, n_col):
-                ctx_copy(1, i).start()
+        return pl.ds(pl.multiple_of(place * length, length), length)
+
+    def cross_copy(way):
+        return send(ctx_own.at[pl.ds(way * half_rows, half_rows), :], relay.at[way],
+                    cross_ss.at[0, way], cross_rs.at[0, way], right if way == 0 else left)
+
+    def relay_copy(way):
+        origin = lax.div(chunk_at(-1 if way == 0 else 1), n_row)
+        at = pl.ds(pl.multiple_of(origin * length + way * half_rows, half_rows), half_rows)
+        return send(relay.at[way], ctx_all.at[at, head_cols],
+                    cross_ss.at[1, way], cross_rs.at[1, way], far_right if way == 0 else far_left)
+
+    def cross_arrives(way):
+        at = pl.ds(pl.multiple_of((1 - b) * length + way * half_rows, half_rows), half_rows)
+        block = ctx_all.at[at, head_cols]
+        send(block, block, cross_ss.at[1, way], cross_rs.at[1, way], far_right).wait_recv()
+
+    def ctx_copies(half):
+        src = ctx_own if half == 0 else ctx_all.at[ctx_rows(1), head_cols]
+        targets = [sibling] + [{"col": lax.rem(c + 2 * i, n_col)} for i in range(1, n_col // 2)]
+        return [
+            send(src, ctx_all.at[ctx_rows(half), head_cols], ctx_ss.at[half, i], ctx_rs.at[half, head], to)
+            for i, to in enumerate(targets)
+        ]
+
+    def ctx_block(half, h):
+        block = ctx_all.at[ctx_rows(half), fixed_cols[h]]
+        return send(block, block, fwd_ss.at[half, h], ctx_rs.at[half, h], sibling)
+
+    def passes_on(h):
+        return jnp.logical_and(core == owner(h) % 2, c != owner(h))
+
+    def ctx_forward(half):
+        for h in range(heads):
+            @pl.when(passes_on(h))
+            def _(h=h):
+                ctx_block(half, h).wait_recv()
+                ctx_block(half, h).start()
 
     def ctx_wait(half):
         for h in range(heads):
-            @pl.when(c != owner(h))
+            @pl.when(core != owner(h) % 2)
             def _(h=h):
-                ctx_arrives(half, h, fixed_cols[h])
+                ctx_block(half, h).wait_recv()
+
+    def cross_start():
+        @pl.when(is_head)
+        def _():
+            for way in range(2):
+                cross_copy(way).start()
+
+    def ctx_start():
+        @pl.when(is_head)
+        def _():
+            for copy in ctx_copies(0):
+                copy.start()
+            ctx_all[ctx_rows(0), head_cols] = ctx_own[...]
+
+    def cross_relay():
+        @pl.when(is_head)
+        def _():
+            for way in range(2):
+                cross_copy(way).wait_recv()
+                relay_copy(way).start()
+
+    def cross_finish():
+        @pl.when(is_head)
+        def _():
+            for way in range(2):
+                cross_arrives(way)
+            for copy in ctx_copies(1):
+                copy.start()
+
+    def ctx_in_order():
+        for slot in range(ring):
+            held = chunk_at(slot - middle)
+            ctx_rel[slot * rows:(slot + 1) * rows, :] = ctx_all[pl.ds(pl.multiple_of(held * rows, rows), rows), :]
 
     def ctx_drain():
         @pl.when(is_head)
         def _():
-            ctx_cross().wait_send()
+            for way in range(2):
+                cross_copy(way).wait_send()
+                relay_copy(way).wait_send()
             for half in range(2):
-                for i in range(1, n_col):
-                    ctx_copy(half, i).wait_send()
+                for copy in ctx_copies(half):
+                    copy.wait_send()
+        for half in range(2):
+            for h in range(heads):
+                @pl.when(passes_on(h))
+                def _(h=h, half=half):
+                    ctx_block(half, h).wait_send()
 
     drain.append(ctx_drain)
 
     def context_grad(offset):
-        block = r + offset
+        block = r + turn * offset
 
         @pl.when(jnp.logical_and(block >= 0, block < n_row))
         def _():
-            held = chunk_at(offset)
+            held = middle + offset
             place = pl.ds(pl.multiple_of(block * rows, rows), rows)
 
             @pl.loop(0, heads // 2)
@@ -248,12 +301,12 @@
                     def _(k=k):
                         cg_recv[c, place, :] = product[:, k * HEAD_DIM:(k + 1) * HEAD_DIM].astype(BF16)
 
-    def context_grads(first, last):
-        if first == 0:
+    def context_grads(step):
+        if step == 0:
             context_grad(0)
-        for step in range(max(first, 1), min(last, n_row - 1) + 1):
+        elif step < n_row:
             @pl.loop(0, 2)
-            def _(way, step=step):
+            def _(way):
                 context_grad((2 * way - 1) * step)
 
     def cg_drain():
@@ -266,14 +319,23 @@
 
     tile = cols // 3
 
-    def project(place):
-        held = chunk_at(place - reach)
-        tokens = ctx_all[pl.ds(pl.multiple_of(held * rows, rows), rows), :]
+    def project(first, last):
+        tokens = ctx_rel[(middle - reach + first) * rows:(middle - reach + last) * rows, :]
 
         @pl.loop(0, 3)
         def _(i):
             at = pl.ds(pl.multiple_of(i * tile, tile), tile)
-            lo[place, :, at] = jnp.dot(tokens, w_ref[:, at], preferred_element_type=F32)
+            product = jnp.dot(tokens, w_ref[:, at], preferred_element_type=F32)
+            lo[first:last, :, at] = product.reshape(last - first, rows, tile)
+
+    def project_ends():
+        project(0, 2)
+        if reach > 1:
+            project(2 * reach - 2, 2 * reach)
+
+    def project_middle():
+        if reach > 2:
+            project(2, 2 * reach - 2)
 
     def out_step(way, step, final=False):
         stage, landed = (rs_stage_r, rs_r) if way == 0 else (rs_stage_l, rs_l)
@@ -295,26 +357,31 @@
 
     def out_both(step):
         if step < reach:
-            project(2 * reach - step)
             out_step(0, step)
         if step <= reach:
-            project(step - 1)
             out_step(1, step)
 
     stripe = cols // n_depth
     part = stripe // 2
 
-    def weight_product(place):
+    def weight_product(place, first, last):
+        at = pl.ds(pl.multiple_of(place * 2 * stripe + b * 128, 128), 256)
+        tokens = grad_all[first:last, :, at].reshape((last - first) * rows, 256)
+        return lax.dot_general(tokens, ctx_rel[first * rows:last * rows, :], TN, preferred_element_type=F32)
+
+    def weight_near():
+        @pl.loop(0, n_y)
+        def _(place):
+            dw_sum[place] = weight_product(place, middle - reach, middle + reach)
+
+    def weight_far(place):
         place = lax.rem(place + 2 * n_y, n_y)
-        at = pl.ds(pl.multiple_of(place * 2 * stripe + b * 128, 128), 256)
-        tokens = grad_all[:, :, at].reshape(ring * rows, 256)
-        dw_full[...] = lax.dot_general(tokens, ctx_all[...], TN, preferred_element_type=F32)
-        dw_sum[place] = dw_full[pl.ds(pl.multiple_of(b * 64, 64), stripe), :]
+        dw_sum[place] += weight_product(place, 0, middle - reach) + weight_product(place, middle + reach, ring)
 
     def weight_step(way, step, final=False):
         place = lax.rem(y + (-step if way == 0 else step) + 2 * n_y, n_y)
         own = slice(way * part, (way + 1) * part)
-        total = dw_sum[place, own, :]
+        total = dw_sum[place, pl.ds(pl.multiple_of(b * 64 + way * part, 32), part), :]
         if step > 1:
             block = dw_recv.at[way, step - 2]
             send(block, block, dw_ss.at[way, step - 2], dw_rs.at[way, step - 2], up).wait_recv()
@@ -373,39 +440,63 @@
 
     drain.append(dqkv_drain)
 
-    last = ring // 2
+    def weight_ends():
+        for way in range(2):
+            if n_y > 2 or way == 0:
+                weight_far(y + 2 * way - 1)
+            weight_step(way, 1)
+
+    def weight_rest():
+        for offset in range(2, n_y - 1):
+            weight_far(y + offset)
+        weight_far(y)
+
+    def weight_both(step):
+        if step < n_y:
+            weight_step(0, step)
+            weight_step(1, step)
+
+    grad_step(1)
+    heads_arrive()
+    forward(0, n_blocks // 2)
+    grad_step(2)
+    forward(n_blocks // 2, n_blocks)
+    cross_start()
+    cross_relay()
+    ctx_start()
     weight_copy.wait()
-    context_grads(0, 1)
-    grad_step(3) if last >= 3 else None
-    context_grads(2, 3)
-    grad_step(4) if last >= 4 else None
-    ctx_relay()
-    context_grads(4, 4)
-    grad_step(5) if last >= 5 else None
+    context_grads(0)
+    context_grads(1)
+    grad_step(3)
+    context_grads(2)
+    grad_step(4)
+    ctx_forward(0)
+    context_grads(3)
+    grad_step(5)
     ctx_wait(0)
+    cross_finish()
+    context_grads(4)
+    grad_step(6)
+    context_grads(5)
+    ctx_forward(1)
+    grad_step(7)
+    context_grads(6)
+    context_grads(7)
     ctx_wait(1)
+    ctx_in_order()
+    project_ends()
+    grad_step(8)
     out_both(1)
-    grad_step(6) if last >= 6 else None
-    context_grads(5, 6)
+    project_middle()
+    weight_near()
     out_both(2)
-    grad_step(7) if last >= 7 else None
-    context_grads(7, n_row)
+    weight_ends()
+    weight_rest()
     out_both(3)
-    for step in range(8, last + 1):
-        grad_step(step)
-    for step in range(4, reach + 1):
-        out_both(step)
-    project(reach)
-    for offset in (-1, 1):
-        weight_product(y + offset)
-        weight_step(0 if offset < 0 else 1, 1)
-    for offset in range(2, n_y - 1):
-        weight_product(y + offset)
-    weight_product(y)
+    weight_both(2)
     backward()
-    for step in range(2, n_y):
-        weight_step(0, step)
-        weight_step(1, step)
+    out_both(4)
+    weight_both(3)
     out_step(0, reach, final=True)
     out_step(1, reach + 1, final=True)
     out_ref[0] = lo[reach].astype(BF16)
@@ -416,10 +507,20 @@
             @pl.when(c != owner(h))
             def _(t=t, h=h):
                 block = dqkv_all.at[t, :, fixed_cols[h]]
-                send(block, block, dq_ss.at[t, 0], dq_rs.at[t, h], other).wait_recv()
+                send(block, block, dq_ss.at[t, 0], dq_rs.at[t, h], sibling).wait_recv()
         ref[0] = dqkv_all[t]
     for wait in drain:
         wait()
+
+
+def hand_over(*refs):
+    count = len(refs) // 2
+    *refs, sem = refs
+    copies = [pltpu.make_async_copy(refs[i], refs[count + i], sem.at[i]) for i in range(count)]
+    for copy in copies:
+        copy.start()
+    for copy in copies:
+        copy.wait()
 
 
 def solution(mesh):
@@ -443,6 +544,8 @@
             pltpu.VMEM((length, length), BF16),
             pltpu.VMEM((length, HEAD_DIM), BF16),
             pltpu.VMEM((HALVES * length, width), BF16),
+            pltpu.VMEM((HALVES * length, width), BF16),
+            pltpu.VMEM((2, length // 2, HEAD_DIM), BF16),
             pltpu.VMEM((ring, rows, cols), BF16),
             pltpu.VMEM((length, width), BF16),
             pltpu.VMEM((n_col, length, HEAD_DIM), BF16),
@@ -454,20 +557,19 @@
             pltpu.VMEM((hops, rows, cols), BF16),
             pltpu.VMEM((hops, rows, cols), BF16),
             pltpu.VMEM((hops, rows, cols), BF16),
-            pltpu.VMEM((256, width), F32),
-            pltpu.VMEM((n_y, stripe, width), F32),
+            pltpu.VMEM((n_y, 256, width), F32),
             pltpu.VMEM((2, turns, stripe // 2, width), BF16),
             pltpu.VMEM((2, turns, stripe // 2, width), BF16),
             dma,
             dma((3, heads)), dma((3, n_col)),
             dma((2, ring // 2, SUBS)), dma((2, ring // 2, SUBS)),
-            dma((2, n_col)), dma((2, heads)),
+            dma((2, n_col)), dma((2, heads)), dma((2, heads)), dma((2, 2)), dma((2, 2)),
             dma((heads,)), dma((n_col,)),
             dma((3, n_col)), dma((3, heads)),
             dma((2, hops, SUBS)), dma((2, hops, SUBS)),
             dma((2, turns)), dma((2, turns)),
         ]
-        layer_out, query_grad, key_grad, value_grad, weight_grad = pl.pallas_call(
+        parts = pl.pallas_call(
             functools.partial(kernel, n_row, n_col, n_depth),
             out_shape=(
                 jax.ShapeDtypeStruct(grad.shape, BF16),
@@ -480,10 +582,19 @@
             out_specs=(vmem,) * 5,
             scratch_shapes=scratch,
             compiler_params=pltpu.CompilerParams(
-                collective_id=0, has_side_effects=True, vmem_limit_bytes=56 * 1024 * 1024
+                collective_id=0, has_side_effects=True, vmem_limit_bytes=VMEM_BYTES
             ),
         )(q, k, v, positions, weight, grad)
-        return layer_out, query_grad, key_grad, value_grad, weight_grad.T
+        anywhere = pl.BlockSpec(memory_space=pltpu.HBM)
+        *parts, weight_grad = pl.pallas_call(
+            hand_over,
+            out_shape=[jax.ShapeDtypeStruct(part.shape, part.dtype) for part in parts],
+            in_specs=[anywhere] * len(parts),
+            out_specs=[anywhere] * len(parts),
+            scratch_shapes=[dma((len(parts),))],
+            compiler_params=pltpu.CompilerParams(vmem_limit_bytes=VMEM_BYTES),
+        )(*parts)
+        return *parts, weight_grad.T
 
     return jax.shard_map(
         local,

time: 111 us -> 130 us (1.17)
  Pallas kernels: 101 us -> 128 us
  local copies, waits for them, and re-layouts: 8.15 us -> 0 us
    pallas_call x0 -> x1, Pallas kernels: none -> 33.9 us  [local(): pl.pallas_call(hand_over, out_shape=[jax.ShapeDtypeStruct(part.shape, par...]
    unnamed x5 -> x0, local copies, waits for them, and re-layouts: 8.15 us -> none
    pallas_call x1, Pallas kernels: 101 us -> 94.2 us  [local(): pl.pallas_call(functools.partial(kernel, n_row, n_col, n_depth), out_shap...]
where the time goes in v2:
time: 130 us; the launch traced here: 129 us
  Pallas kernels  128 us (98%)
    pallas_call x1, Pallas kernels, local(): pl.pallas_call(functools.partial(kernel, n_row, n_col, n_depth), out_shap...  94.2 us
    pallas_call x1, Pallas kernels, local(): pl.pallas_call(hand_over, out_shape=[jax.ShapeDtypeStruct(part.shape, par...  33.9 us

profile of v2, /device:TPU:24, one launch (start us, length us, event | category | flops | bytes accessed | tf_op | source)
XLA Modules:
  0.0 128.8 jit_solution(3962304249896774144)
XLA Ops:
  0.6 94.2 %shard_map.101 = (bf16[1,64,1536]{2,1,0:T(8,128)(2,1)}, bf16[1,64,768]{2,1,0:T(8,128)(2,1)}, bf16[1,64,768]{2,1,0:T(8,128)(2,1)}, bf16[1,64,768]{2,1,0:T(8,128)(2,1)}, f32[192,768]{1,0:T(8,128)}) custom-call(bf16[1,64,768]{2,1,0:T(8,128)(2,1)} %q_ref.1, bf16[1,64,768]{2,1,0:T(8,128)(2,1)} %k_ref.1, bf16[1,64,768]{2,1,0:T(8,128)(2,1)} %v_ref.1, ...), custom_call_target="tpu_custom_call" | custom-call | tf_op jit(solution)/shard_map/pallas_call | solution.py:572
  94.9 33.9 %shard_map.102 = (bf16[1,64,1536]{2,1,0:T(8,128)(2,1)}, bf16[1,64,768]{2,1,0:T(8,128)(2,1)}, bf16[1,64,768]{2,1,0:T(8,128)(2,1)}, bf16[1,64,768]{2,1,0:T(8,128)(2,1)}, f32[192,768]{1,0:T(8,128)}) custom-call(bf16[1,64,1536]{2,1,0:T(8,128)(2,1)} %get-tuple-element.15.refs_0_, bf16[1,64,768]{2,1,0:T(8,128)(2,1)} %get-tuple-element.16.refs_1_, ...), custom_call_target="tpu_custom_call" | custom-call | tf_op jit(solution)/shard_map/pallas_call | solution.py:589

commit v3 on v2

v3 whole, which is shorter than its diff:
```python
import functools

import jax
import jax.numpy as jnp
from jax import lax
from jax.experimental import pallas as pl
from jax.experimental.pallas import tpu as pltpu
from jax.sharding import PartitionSpec as P

HEAD_DIM = 128
HALVES = 2
THIRDS = 3
SUBS = 2
LANES = 128
VMEM_BYTES = 56 * 1024 * 1024
MESH = pl.DeviceIdType.MESH
F32, BF16 = jnp.float32, jnp.bfloat16

NT = (((1,), (1,)), ((), ()))
TN = (((0,), (0,)), ((), ()))


def kernel(
    n_row, n_col, n_depth,
    q_ref, k_ref, v_ref, pos_ref, w_hbm, g_ref,
    out_ref, dq_ref, dk_ref, dv_ref, dw_ref,
    w_ref, qkv_stage, qkv, pos_col, probs, probs_b, dlogits, ctx_own, ctx_all, ctx_rel, relay, grad_all,
    cg_stage, cg_recv, cg_near, cg_own, dqkv_own, dqkv_all,
    lo, rs_stage_r, rs_stage_l, rs_r, rs_l, dw_sum, dw_stage, dw_recv,
    w_sem, qkv_ss, qkv_rs, ag_ss, ag_rs, ctx_ss, ctx_rs, fwd_ss, cross_ss, cross_rs, cg_ss, cg_rs, cgx_ss, cgx_rs, dq_ss, dq_rs,
    rs_ss, rs_rs, dw_ss, dw_rs,
):
    r, c, d = lax.axis_index("row"), lax.axis_index("col"), lax.axis_index("depth")
    y, b = lax.div(d, HALVES), lax.rem(d, HALVES)
    ring, n_y = HALVES * n_row, n_depth // HALVES
    reach = n_row // 2
    z = b * n_row + r
    span, width = q_ref.shape[1:]
    rows, cols = g_ref.shape[1:]
    length = pos_ref.shape[1]
    heads = width // HEAD_DIM
    scale = HEAD_DIM ** (-0.5)

    def on_ring(place):
        place = lax.rem(place + 2 * ring, ring)
        return {"row": lax.rem(place, n_row), "depth": y * HALVES + lax.div(place, n_row)}

    def on_y(place):
        return {"depth": lax.rem(place + n_y, n_y) * HALVES + b}

    def chunk_at(offset):
        return lax.rem(z + offset + 2 * ring, ring)

    def owner(h):
        return (h * n_col) // heads

    core = lax.rem(c, 2)
    right, left, up, down = on_ring(z + 1), on_ring(z - 1), on_y(y + 1), on_y(y - 1)
    sibling = {"col": c + 1 - 2 * core}
    far_right, far_left, other = on_ring(z + n_row - 1), on_ring(z - n_row + 1), on_ring(z + n_row)
    middle = ring // 2
    head, is_head = 0, c == owner(0)
    for h in range(1, heads):
        head = jnp.where(c >= owner(h), h, head)
        is_head = jnp.logical_or(is_head, c == owner(h))
    head_cols = pl.ds(pl.multiple_of(head * HEAD_DIM, HEAD_DIM), HEAD_DIM)
    fixed_cols = [pl.ds(h * HEAD_DIM, HEAD_DIM) for h in range(heads)]
    sub_cols = [pl.ds(u * (cols // SUBS), cols // SUBS) for u in range(SUBS)]

    def send(src, dst, send_sem, recv_sem, to):
        return pltpu.make_async_remote_copy(
            src_ref=src, dst_ref=dst, send_sem=send_sem, recv_sem=recv_sem,
            device_id=to, device_id_type=MESH,
        )

    def wait_bytes(ref, sem):
        pltpu.make_async_copy(ref, ref, sem).wait()

    barrier = pltpu.get_barrier_semaphore()
    peers = [{"col": lax.rem(c + i, n_col)} for i in range(1, n_col)]
    peers += [right, left, other, up]
    if n_y > 2:
        peers += [down]
    if n_row > 2:
        peers += [far_right, far_left]
    for peer in peers:
        pl.semaphore_signal(barrier, inc=1, device_id=peer, device_id_type=MESH)
    third = cols // THIRDS
    tiles = [(pl.ds((n * THIRDS + t) * LANES, LANES), pl.ds(t * third + n * LANES, LANES))
             for n in range(n_y) for t in range(THIRDS)]
    weight_copies = [pltpu.make_async_copy(w_hbm.at[:, given], w_ref.at[:, held], w_sem.at[i])
                     for i, (given, held) in enumerate(tiles)]
    for copy in weight_copies:
        copy.start()
    for given, held in tiles:
        grad_all[middle, :, held] = g_ref[0, :, given]
    pl.semaphore_wait(barrier, len(peers))

    drain = []

    far = [ring // 2, ring // 2 - 1]
    near = [reach, reach - 1]
    third_cols = [pl.ds(u * third, third) for u in range(THIRDS)]

    def grad_copy(way, step, u):
        sign = -1 if way == 0 else 1
        return send(grad_all.at[middle + sign * (step - 1), :, third_cols[u]],
                    grad_all.at[middle + sign * step, :, third_cols[u]],
                    ag_ss.at[way, step - 1, u], ag_rs.at[way, step - 1, u], right if way == 0 else left)

    def where_needed(place, way, step, u, action):
        if step <= near[way] or u == 1:
            action()
            return
        place = lax.rem(place + ring, ring)
        line, half = lax.rem(place, n_row), lax.div(place, n_row)
        onward = far[way] - step
        crosses = line + onward >= n_row if way == 0 else line - onward < 0
        pl.when(jnp.logical_or(crosses, half == (0 if u == 0 else 1)))(action)

    def grad_start(way, step, u):
        where_needed(z + (1 if way == 0 else -1), way, step, u, grad_copy(way, step, u).start)

    def grad_step(step):
        for u in (1, 0, 2):
            for way in range(2):
                if step <= far[way]:
                    def pass_on(way=way, u=u):
                        grad_copy(way, step, u).wait_recv()
                        if step < far[way]:
                            grad_start(way, step + 1, u)

                    where_needed(z, way, step, u, pass_on)

    def grad_drain():
        for way in range(2):
            for step in range(1, far[way] + 1):
                for u in range(THIRDS):
                    where_needed(z + (1 if way == 0 else -1), way, step, u, grad_copy(way, step, u).wait_send)

    drain.append(grad_drain)
    for u in (1, 0, 2):
        for way in range(2):
            grad_start(way, 1, u)

    own_span = pl.ds(pl.multiple_of(c * span, span), span)
    for t, ref in enumerate((q_ref, k_ref, v_ref)):
        qkv_stage[t] = ref[0]

    def heads_copy(h):
        return send(qkv_stage.at[:, :, fixed_cols[h]], qkv.at[:, own_span, :],
                    qkv_ss.at[h], qkv_rs.at[c], {"col": owner(h)})

    for h in range(heads):
        @pl.when(c != owner(h))
        def _(h=h):
            heads_copy(h).start()

    @pl.when(is_head)
    def _():
        for t in range(3):
            qkv[t, own_span, :] = qkv_stage[t, :, head_cols]

    def heads_drain():
        for h in range(heads):
            @pl.when(c != owner(h))
            def _(h=h):
                heads_copy(h).wait_send()

    drain.append(heads_drain)

    block_rows = min(128, length)

    def forward(first, last):
        @pl.when(is_head)
        def _():
            for i in range(first, last):
                at = pl.ds(i * block_rows, block_rows)
                logits = lax.dot_general(qkv[0, at, :], qkv[1], NT, preferred_element_type=F32)
                visible = pos_ref[...].astype(F32) <= pos_col[at, 0:1]
                logits = jnp.where(visible, logits * scale, -jnp.inf)
                highest = jnp.max(logits, axis=-1, keepdims=True)
                grown = jnp.exp(logits - highest)
                prob = grown / jnp.sum(grown, axis=-1, keepdims=True)
                probs[at, :] = prob
                rounded = prob.astype(BF16)
                probs_b[at, :] = rounded
                context = jnp.dot(rounded, qkv[2], preferred_element_type=F32)
                ctx_own[at, :] = context.astype(BF16)

    n_blocks = length // block_rows

    def heads_arrive():
        @pl.when(is_head)
        def _():
            pos_col[...] = jnp.transpose(
                jnp.broadcast_to(pos_ref[...].astype(F32), (128, length))
            )
            for i in range(1, n_col):
                src = lax.rem(c + i, n_col)
                place = qkv.at[:, pl.ds(pl.multiple_of(src * span, span), span), :]
                send(place, place, qkv_ss.at[0], qkv_rs.at[src], {"col": src}).wait_recv()

    half_rows, quarter = length // 2, length // 4

    def ctx_rows(group):
        if group == 0:
            return pl.ds(pl.multiple_of(b * length, length), length)
        return crossing_rows(1 - b, r, group - 1)

    def crossing_rows(place, line, phase):
        start = place * length + jnp.where(line < reach, 1 - phase, phase) * half_rows
        return pl.ds(pl.multiple_of(start, half_rows), half_rows)

    def crossing_part(place, line, phase, way):
        start = place * length + jnp.where(line < reach, 1 - phase, phase) * half_rows + way * quarter
        return pl.ds(pl.multiple_of(start, quarter), quarter)

    def cross_copy(phase, way):
        return send(ctx_own.at[crossing_part(0, r, phase, way), :], relay.at[phase, way],
                    cross_ss.at[0, phase, way], cross_rs.at[0, phase, way], right if way == 0 else left)

    def relay_copy(phase, way):
        origin = chunk_at(-1 if way == 0 else 1)
        at = crossing_part(lax.div(origin, n_row), lax.rem(origin, n_row), phase, way)
        return send(relay.at[phase, way], ctx_all.at[at, head_cols],
                    cross_ss.at[1, phase, way], cross_rs.at[1, phase, way], far_right if way == 0 else far_left)

    def cross_arrives(phase, way):
        block = ctx_all.at[crossing_part(1 - b, r, phase, way), head_cols]
        send(block, block, cross_ss.at[1, phase, way], cross_rs.at[1, phase, way], far_right).wait_recv()

    def ctx_copies(group):
        src = ctx_own if group == 0 else ctx_all.at[ctx_rows(group), head_cols]
        targets = [sibling] + [{"col": lax.rem(c + 2 * i, n_col)} for i in range(1, n_col // 2)]
        return [
            send(src, ctx_all.at[ctx_rows(group), head_cols], ctx_ss.at[group, i], ctx_rs.at[group, head], to)
            for i, to in enumerate(targets)
        ]

    def ctx_block(half, h):
        block = ctx_all.at[ctx_rows(half), fixed_cols[h]]
        return send(block, block, fwd_ss.at[half, h], ctx_rs.at[half, h], sibling)

    def passes_on(h):
        return jnp.logical_and(core == owner(h) % 2, c != owner(h))

    def ctx_forward(half):
        for h in range(heads):
            @pl.when(passes_on(h))
            def _(h=h):
                ctx_block(half, h).wait_recv()
                ctx_block(half, h).start()

    def ctx_wait(half):
        for h in range(heads):
            @pl.when(core != owner(h) % 2)
            def _(h=h):
                ctx_block(half, h).wait_recv()

    def cross_start():
        @pl.when(is_head)
        def _():
            for phase in range(2):
                for way in range(2):
                    cross_copy(phase, way).start()

    def ctx_start():
        @pl.when(is_head)
        def _():
            for copy in ctx_copies(0):
                copy.start()
            ctx_all[ctx_rows(0), head_cols] = ctx_own[...]

    def cross_relay():
        @pl.when(is_head)
        def _():
            for phase in range(2):
                for way in range(2):
                    cross_copy(phase, way).wait_recv()
                    relay_copy(phase, way).start()

    def cross_finish(phase):
        @pl.when(is_head)
        def _():
            for way in range(2):
                cross_arrives(phase, way)
            for copy in ctx_copies(1 + phase):
                copy.start()

    def ctx_in_order(first, last):
        for slot in range(first, last):
            held = chunk_at(slot - middle)
            ctx_rel[slot * rows:(slot + 1) * rows, :] = ctx_all[pl.ds(pl.multiple_of(held * rows, rows), rows), :]

    def ctx_drain():
        @pl.when(is_head)
        def _():
            for phase in range(2):
                for way in range(2):
                    cross_copy(phase, way).wait_send()
                    relay_copy(phase, way).wait_send()
            for group in range(3):
                for copy in ctx_copies(group):
                    copy.wait_send()
        for group in range(3):
            for h in range(heads):
                @pl.when(passes_on(h))
                def _(h=h, group=group):
                    ctx_block(group, h).wait_send()

    drain.append(ctx_drain)

    inner = reach // 2
    near_parts = [(reach - inner, 2 * inner), (0, reach - inner), (reach + inner, reach - inner)]

    def near_copy(part, h):
        at = pl.ds(near_parts[part][0] * rows, near_parts[part][1] * rows)
        return send(cg_stage.at[at, fixed_cols[h]], cg_recv.at[c, at, :],
                    cg_ss.at[part, h], cg_rs.at[part, c], {"col": owner(h)})

    def context_grads(parts):
        parts = [part for part in parts if near_parts[part][1] > 0]
        if not parts:
            return
        tokens = []
        for part in parts:
            first, count = near_parts[part]
            slots = grad_all[middle - reach + first:middle - reach + first + count]
            tokens.append(slots.reshape(count * rows, cols))
        tokens = tokens[0] if len(tokens) == 1 else jnp.concatenate(tokens, axis=0)
        for i in range(heads // 2):
            two = pl.ds(i * 2 * HEAD_DIM, 2 * HEAD_DIM)
            product = lax.dot_general(tokens, w_ref[two, :], NT, preferred_element_type=F32).astype(BF16)
            done = 0
            for part in parts:
                first, count = near_parts[part]
                cg_stage[first * rows:(first + count) * rows, two] = product[done:done + count * rows]
                done += count * rows
            for h in (2 * i, 2 * i + 1):
                @pl.when(c != owner(h))
                def _(h=h):
                    for part in parts:
                        near_copy(part, h).start()

    def near_sum():
        @pl.when(is_head)
        def _():
            cg_recv[c] = cg_stage[:, head_cols]
            for i in range(1, n_col):
                src = lax.rem(c + i, n_col)
                for part, (first, count) in enumerate(near_parts):
                    if count > 0:
                        block = cg_recv.at[src, pl.ds(first * rows, count * rows), :]
                        send(block, block, cg_ss.at[part, 0], cg_rs.at[part, src], {"col": src}).wait_recv()
            for i in range(2 * reach):
                at = pl.ds(i * rows, rows)
                total = cg_recv[0, at, :].astype(F32)
                for k in range(1, n_col):
                    total = total + cg_recv[k, at, :].astype(F32)
                cg_near[at, :] = total.astype(BF16)
            for i in range(2 * reach):
                @pl.when(is_own(i))
                def _(i=i):
                    cg_own[near_rows(i), :] = cg_near[i * rows:(i + 1) * rows, :]

                @pl.when(jnp.logical_not(is_own(i)))
                def _(i=i):
                    near_cross(i).start()

    def is_own(i):
        block = r + i - reach
        return jnp.logical_and(block >= 0, block < n_row)

    def near_block(i):
        return lax.rem(r + i - reach + n_row, n_row)

    def near_rows(i):
        return pl.ds(pl.multiple_of(near_block(i) * rows, rows), rows)

    def near_cross(i):
        return send(cg_near.at[pl.ds(i * rows, rows), :], cg_own.at[near_rows(i), :],
                    cgx_ss.at[i], cgx_rs.at[near_block(i)], other)

    def cross_wait():
        for block in range(n_row):
            offset = block - r

            @pl.when(jnp.logical_or(offset < -reach, offset >= reach))
            def _(block=block):
                at = cg_own.at[pl.ds(block * rows, rows), :]
                send(at, at, cgx_ss.at[0], cgx_rs.at[block], other).wait_recv()

    def cg_drain():
        for part, (_, count) in enumerate(near_parts):
            if count > 0:
                for h in range(heads):
                    @pl.when(c != owner(h))
                    def _(part=part, h=h):
                        near_copy(part, h).wait_send()
        for i in range(2 * reach):
            @pl.when(jnp.logical_and(is_head, jnp.logical_not(is_own(i))))
            def _(i=i):
                near_cross(i).wait_send()

    drain.append(cg_drain)

    tile = cols // 3

    def project(first, last):
        tokens = ctx_rel[(middle - reach + first) * rows:(middle - reach + last) * rows, :]

        @pl.loop(0, 3)
        def _(i):
            at = pl.ds(pl.multiple_of(i * tile, tile), tile)
            product = jnp.dot(tokens, w_ref[:, at], preferred_element_type=F32)
            lo[first:last, :, at] = product.reshape(last - first, rows, tile)

    def project_ends():
        project(0, 2)
        if reach > 1:
            project(2 * reach - 2, 2 * reach)

    def project_middle():
        if reach > 2:
            project(2, 2 * reach - 2)

    def out_step(way, step, final=False):
        stage, landed = (rs_stage_r, rs_r) if way == 0 else (rs_stage_l, rs_l)
        place = (2 * reach - step) if way == 0 else step - 1
        for u in range(SUBS):
            total = lo[place, :, sub_cols[u]]
            if step > 1:
                block = landed.at[step - 2, :, sub_cols[u]]
                send(block, block, rs_ss.at[way, step - 2, u], rs_rs.at[way, step - 2, u], right).wait_recv()
                total = total + block[...].astype(F32)
            if final:
                lo[place, :, sub_cols[u]] = total
                continue
            stage[step - 1, :, sub_cols[u]] = total.astype(BF16)
            copy = send(stage.at[step - 1, :, sub_cols[u]], landed.at[step - 1, :, sub_cols[u]],
                        rs_ss.at[way, step - 1, u], rs_rs.at[way, step - 1, u], right if way == 0 else left)
            copy.start()
            drain.append(copy.wait_send)

    def out_both(step):
        if step < reach:
            out_step(0, step)
        if step <= reach:
            out_step(1, step)

    stripe = cols // n_depth
    part = stripe // 2

    def weight_product(place, first, last):
        pair = [
            grad_all[first:last, :, pl.ds(pl.multiple_of((b + i) * third + place * LANES, LANES), LANES)]
            for i in range(2)
        ]
        tokens = jnp.concatenate(pair, axis=-1).reshape((last - first) * rows, 2 * LANES)
        return lax.dot_general(tokens, ctx_rel[first * rows:last * rows, :], TN, preferred_element_type=F32)

    def weight_near(first, last):
        @pl.loop(first, last)
        def _(place):
            dw_sum[place] = weight_product(place, middle - reach, middle + reach)

    def weight_far(place):
        place = lax.rem(place + 2 * n_y, n_y)
        dw_sum[place] += weight_product(place, 0, middle - reach) + weight_product(place, middle + reach, ring)

    def weight_step(way, step, final=False):
        place = lax.rem(y + (-step if way == 0 else step) + 2 * n_y, n_y)
        own = slice(way * part, (way + 1) * part)
        total = dw_sum[place, pl.ds(pl.multiple_of(b * 64 + way * part, 32), part), :]
        if step > 1:
            block = dw_recv.at[way, step - 2]
            send(block, block, dw_ss.at[way, step - 2], dw_rs.at[way, step - 2], up).wait_recv()
            total = total + block[...].astype(F32)
        if final:
            dw_ref[own, :] = total
            return
        dw_stage[way, step - 1] = total.astype(BF16)
        copy = send(dw_stage.at[way, step - 1], dw_recv.at[way, step - 1], dw_ss.at[way, step - 1],
                    dw_rs.at[way, step - 1], up if way == 0 else down)
        copy.start()
        drain.append(copy.wait_send)

    def backward():
        @pl.when(is_head)
        def _():
            cross_wait()
            for i in range(n_blocks):
                at = pl.ds(i * block_rows, block_rows)
                grad = cg_own[at, :]
                row_dot = jnp.sum(grad.astype(F32) * ctx_own[at, :].astype(F32), axis=-1, keepdims=True)
                dprob = lax.dot_general(grad, qkv[2], NT, preferred_element_type=F32)
                rounded = (probs[at, :] * (dprob - row_dot)).astype(BF16)
                dlogits[at, :] = rounded
                query_grad = jnp.dot(rounded, qkv[1], preferred_element_type=F32) * scale
                dqkv_own[0, at, :] = query_grad.astype(BF16)
            key_grad = lax.dot_general(dlogits[...], qkv[0], TN, preferred_element_type=F32) * scale
            dqkv_own[1] = key_grad.astype(BF16)
            value_grad = lax.dot_general(probs_b[...], cg_own[...], TN, preferred_element_type=F32)
            dqkv_own[2] = value_grad.astype(BF16)
            for i in range(1, n_col):
                dqkv_copy(i).start()
            for t in range(3):
                dqkv_all[t, :, head_cols] = dqkv_own[t, own_span, :]

    def dqkv_copy(i):
        to = lax.rem(c + i, n_col)
        return send(dqkv_own.at[:, pl.ds(pl.multiple_of(to * span, span), span), :],
                    dqkv_all.at[:, :, head_cols], dq_ss.at[i], dq_rs.at[head], {"col": to})

    def dqkv_drain():
        @pl.when(is_head)
        def _():
            for i in range(1, n_col):
                dqkv_copy(i).wait_send()

    drain.append(dqkv_drain)

    def weight_ends():
        for way in range(2):
            if n_y > 2 or way == 0:
                weight_far(y + 2 * way - 1)
            weight_step(way, 1)

    def weight_rest():
        for offset in range(2, n_y - 1):
            weight_far(y + offset)
        weight_far(y)

    def weight_both(step):
        if step < n_y:
            weight_step(0, step)
            weight_step(1, step)

    def dqkv_finish():
        for h in range(heads):
            @pl.when(c != owner(h))
            def _(h=h):
                block = dqkv_all.at[:, :, fixed_cols[h]]
                send(block, block, dq_ss.at[0], dq_rs.at[h], sibling).wait_recv()
        for t, ref in enumerate((dq_ref, dk_ref, dv_ref)):
            ref[0] = dqkv_all[t]

    grad_step(1)
    heads_arrive()
    forward(0, n_blocks // 2)
    grad_step(2)
    forward(n_blocks // 2, n_blocks)
    cross_start()
    cross_relay()
    ctx_start()
    cross_finish(0)
    grad_step(3)
    for copy in weight_copies:
        copy.wait()
    context_grads([0])
    ctx_forward(0)
    grad_step(4)
    context_grads([1, 2])
    ctx_wait(0)
    ctx_forward(1)
    grad_step(5)
    ctx_wait(1)
    ctx_in_order(middle - reach, middle + reach)
    project_ends()
    out_both(1)
    weight_near(0, n_y // 2)
    grad_step(6)
    out_both(2)
    project_middle()
    near_sum()
    cross_finish(1)
    grad_step(7)
    ctx_forward(2)
    weight_near(n_y // 2, n_y)
    out_both(3)
    grad_step(8)
    ctx_wait(2)
    ctx_in_order(0, middle - reach)
    ctx_in_order(middle + reach, ring)
    weight_ends()
    weight_rest()
    out_both(4)
    weight_both(2)
    backward()
    weight_both(3)
    out_step(0, reach, final=True)
    out_step(1, reach + 1, final=True)
    for given, held in tiles:
        out_ref[0, :, given] = lo[reach, :, held].astype(BF16)
    weight_step(0, n_y, final=True)
    weight_step(1, n_y, final=True)
    dqkv_finish()
    for wait in drain:
        wait()


def hand_over(*refs):
    count = len(refs) // 3
    parts, outs, held = refs[:count], refs[count:2 * count], refs[2 * count:3 * count]
    sem = refs[-1]
    inward = [pltpu.make_async_copy(parts[i], held[i], sem.at[0, i]) for i in range(count)]
    outward = [pltpu.make_async_copy(held[i], outs[i], sem.at[1, i]) for i in range(count)]
    for copy in inward:
        copy.start()
    for i in range(count):
        inward[i].wait()
        outward[i].start()
    for copy in outward:
        copy.wait()


def solution(mesh):
    n_row, n_col, n_depth = mesh.shape["row"], mesh.shape["col"], mesh.shape["depth"]

    def local(q, k, v, positions, weight, grad):
        _, span, width = q.shape
        _, rows, cols = grad.shape
        length = positions.shape[1]
        heads, ring, reach, n_y = width // HEAD_DIM, HALVES * n_row, n_row // 2, n_depth // HALVES
        stripe = cols // n_depth
        vmem = pl.BlockSpec(memory_space=pltpu.VMEM)
        dma = pltpu.SemaphoreType.DMA
        hops, turns = max(reach, 1), max(n_y - 1, 1)
        scratch = [
            pltpu.VMEM((width, cols), BF16),
            pltpu.VMEM((3, span, width), BF16),
            pltpu.VMEM((3, length, HEAD_DIM), BF16),
            pltpu.VMEM((length, 128), F32),
            pltpu.VMEM((length, length), F32),
            pltpu.VMEM((length, length), BF16),
            pltpu.VMEM((length, length), BF16),
            pltpu.VMEM((length, HEAD_DIM), BF16),
            pltpu.VMEM((HALVES * length, width), BF16),
            pltpu.VMEM((HALVES * length, width), BF16),
            pltpu.VMEM((2, 2, length // 4, HEAD_DIM), BF16),
            pltpu.VMEM((ring, rows, cols), BF16),
            pltpu.VMEM((length, width), BF16),
            pltpu.VMEM((n_col, length, HEAD_DIM), BF16),
            pltpu.VMEM((length, HEAD_DIM), BF16),
            pltpu.VMEM((length, HEAD_DIM), BF16),
            pltpu.VMEM((3, length, HEAD_DIM), BF16),
            pltpu.VMEM((3, span, width), BF16),
            pltpu.VMEM((2 * reach, rows, cols), F32),
            pltpu.VMEM((hops, rows, cols), BF16),
            pltpu.VMEM((hops, rows, cols), BF16),
            pltpu.VMEM((hops, rows, cols), BF16),
            pltpu.VMEM((hops, rows, cols), BF16),
            pltpu.VMEM((n_y, 256, width), F32),
            pltpu.VMEM((2, turns, stripe // 2, width), BF16),
            pltpu.VMEM((2, turns, stripe // 2, width), BF16),
            dma((THIRDS * n_y,)),
            dma((heads,)), dma((n_col,)),
            dma((2, ring // 2, THIRDS)), dma((2, ring // 2, THIRDS)),
            dma((3, n_col)), dma((3, heads)), dma((3, heads)), dma((2, 2, 2)), dma((2, 2, 2)),
            dma((3, heads)), dma((3, n_col)), dma((2 * reach,)), dma((n_row,)),
            dma((n_col,)), dma((heads,)),
            dma((2, hops, SUBS)), dma((2, hops, SUBS)),
            dma((2, turns)), dma((2, turns)),
        ]
        parts = pl.pallas_call(
            functools.partial(kernel, n_row, n_col, n_depth),
            out_shape=(
                jax.ShapeDtypeStruct(grad.shape, BF16),
                jax.ShapeDtypeStruct(q.shape, BF16),
                jax.ShapeDtypeStruct(k.shape, BF16),
                jax.ShapeDtypeStruct(v.shape, BF16),
                jax.ShapeDtypeStruct((stripe, width), F32),
            ),
            in_specs=[vmem] * 4 + [pl.BlockSpec(memory_space=pl.ANY), vmem],
            out_specs=(vmem,) * 5,
            scratch_shapes=scratch,
            compiler_params=pltpu.CompilerParams(
                collective_id=0, has_side_effects=True, vmem_limit_bytes=VMEM_BYTES
            ),
        )(q, k, v, positions, weight, grad)
        anywhere = pl.BlockSpec(memory_space=pltpu.HBM)
        *parts, weight_grad = pl.pallas_call(
            hand_over,
            out_shape=[jax.ShapeDtypeStruct(part.shape, part.dtype) for part in parts],
            in_specs=[anywhere] * len(parts),
            out_specs=[anywhere] * len(parts),
            scratch_shapes=[pltpu.VMEM(part.shape, part.dtype) for part in parts] + [dma((2, len(parts)))],
            compiler_params=pltpu.CompilerParams(vmem_limit_bytes=VMEM_BYTES),
        )(*parts)
        return *parts, weight_grad.T

    return jax.shard_map(
        local,
        mesh=mesh,
        in_specs=(
            P("depth", "col", "row"),
            P("depth", "col", "row"),
            P("depth", "col", "row"),
            P("depth", None),
            P("row", "col"),
            P("depth", "row", "col"),
        ),
        out_specs=(
            P("depth", "row", "col"),
            P("depth", "col", "row"),
            P("depth", "col", "row"),
            P("depth", "col", "row"),
            P("row", ("col", "depth")),
        ),
        check_vma=False,
    )
```

time: 130 us -> 98 us (0.75)
  the two profiles are of different devices: /device:TPU:24 before, /device:TPU:36 now
where the time goes in v3:
time: 98 us; the launch traced here: 97.9 us
  Pallas kernels  97.2 us (99%)
    pallas_call x1, Pallas kernels, local(): pl.pallas_call(functools.partial(kernel, n_row, n_col, n_depth), out_shap...  95 us
    pallas_call x1, Pallas kernels, local(): pl.pallas_call(hand_over, out_shape=[jax.ShapeDtypeStruct(part.shape, par...  2.22 us

profile of v3, /device:TPU:36, one launch (start us, length us, event | category | flops | bytes accessed | tf_op | source)
XLA Modules:
  0.0 97.9 jit_solution(14030003778297275186)
XLA Ops:
  0.6 95.0 %shard_map.101 = (bf16[1,64,1536]{2,1,0:T(8,128)(2,1)}, bf16[1,64,768]{2,1,0:T(8,128)(2,1)}, bf16[1,64,768]{2,1,0:T(8,128)(2,1)}, bf16[1,64,768]{2,1,0:T(8,128)(2,1)}, f32[192,768]{1,0:T(8,128)}) custom-call(bf16[1,64,768]{2,1,0:T(8,128)(2,1)} %q_ref.1, bf16[1,64,768]{2,1,0:T(8,128)(2,1)} %k_ref.1, bf16[1,64,768]{2,1,0:T(8,128)(2,1)} %v_ref.1, ...), custom_call_target="tpu_custom_call" | custom-call | tf_op jit(solution)/shard_map/pallas_call | solution.py:666
  95.7 2.2 %shard_map.102 = (bf16[1,64,1536]{2,1,0:T(8,128)(2,1)}, bf16[1,64,768]{2,1,0:T(8,128)(2,1)}, bf16[1,64,768]{2,1,0:T(8,128)(2,1)}, bf16[1,64,768]{2,1,0:T(8,128)(2,1)}, f32[192,768]{1,0:T(8,128)}) custom-call(bf16[1,64,1536]{2,1,0:T(8,128)(2,1)} %get-tuple-element.15.refs_0_, bf16[1,64,768]{2,1,0:T(8,128)(2,1)} %get-tuple-element.16.refs_1_, ...), custom_call_target="tpu_custom_call" | custom-call | tf_op jit(solution)/shard_map/pallas_call | solution.py:683

commit v4 on v3

--- a/solution.py
+++ b/solution.py
@@ -27,7 +27,7 @@
     w_ref, qkv_stage, qkv, pos_col, probs, probs_b, dlogits, ctx_own, ctx_all, ctx_rel, relay, grad_all,
     cg_stage, cg_recv, cg_near, cg_own, dqkv_own, dqkv_all,
     lo, rs_stage_r, rs_stage_l, rs_r, rs_l, dw_sum, dw_stage, dw_recv,
-    w_sem, qkv_ss, qkv_rs, ag_ss, ag_rs, ctx_ss, ctx_rs, fwd_ss, cross_ss, cross_rs, cg_ss, cg_rs, cgx_ss, cgx_rs, dq_ss, dq_rs,
+    w_sem, g_sem, in_sem, qkv_ss, qkv_rs, ag_ss, ag_rs, ctx_ss, ctx_rs, cross_ss, cross_rs, cg_ss, cg_rs, cgx_ss, cgx_rs, dq_ss, dq_rs,
     rs_ss, rs_rs, dw_ss, dw_rs,
 ):
     r, c, d = lax.axis_index("row"), lax.axis_index("col"), lax.axis_index("depth")
@@ -54,9 +54,7 @@
     def owner(h):
         return (h * n_col) // heads
 
-    core = lax.rem(c, 2)
     right, left, up, down = on_ring(z + 1), on_ring(z - 1), on_y(y + 1), on_y(y - 1)
-    sibling = {"col": c + 1 - 2 * core}
     far_right, far_left, other = on_ring(z + n_row - 1), on_ring(z - n_row + 1), on_ring(z + n_row)
     middle = ring // 2
     head, is_head = 0, c == owner(0)
@@ -72,9 +70,6 @@
             src_ref=src, dst_ref=dst, send_sem=send_sem, recv_sem=recv_sem,
             device_id=to, device_id_type=MESH,
         )
-
-    def wait_bytes(ref, sem):
-        pltpu.make_async_copy(ref, ref, sem).wait()
 
     barrier = pltpu.get_barrier_semaphore()
     peers = [{"col": lax.rem(c + i, n_col)} for i in range(1, n_col)]
@@ -90,13 +85,17 @@
              for n in range(n_y) for t in range(THIRDS)]
     weight_copies = [pltpu.make_async_copy(w_hbm.at[:, given], w_ref.at[:, held], w_sem.at[i])
                      for i, (given, held) in enumerate(tiles)]
-    for copy in weight_copies:
+    head_copies = [pltpu.make_async_copy(ref.at[0], qkv_stage.at[t], in_sem.at[t])
+                   for t, ref in enumerate((q_ref, k_ref, v_ref))]
+    grad_copies = [pltpu.make_async_copy(g_ref.at[0, :, given], grad_all.at[middle, :, held], g_sem.at[i])
+                   for i, (given, held) in enumerate(tiles)]
+    for copy in grad_copies + head_copies + weight_copies:
         copy.start()
-    for given, held in tiles:
-        grad_all[middle, :, held] = g_ref[0, :, given]
+    for copy in grad_copies + head_copies:
+        copy.wait()
     pl.semaphore_wait(barrier, len(peers))
 
-    drain = []
+    drain, late = [], []
 
     far = [ring // 2, ring // 2 - 1]
     near = [reach, reach - 1]
@@ -144,9 +143,6 @@
             grad_start(way, 1, u)
 
     own_span = pl.ds(pl.multiple_of(c * span, span), span)
-    for t, ref in enumerate((q_ref, k_ref, v_ref)):
-        qkv_stage[t] = ref[0]
-
     def heads_copy(h):
         return send(qkv_stage.at[:, :, fixed_cols[h]], qkv.at[:, own_span, :],
                     qkv_ss.at[h], qkv_rs.at[c], {"col": owner(h)})
@@ -181,7 +177,7 @@
                 logits = jnp.where(visible, logits * scale, -jnp.inf)
                 highest = jnp.max(logits, axis=-1, keepdims=True)
                 grown = jnp.exp(logits - highest)
-                prob = grown / jnp.sum(grown, axis=-1, keepdims=True)
+                prob = grown * (1.0 / jnp.sum(grown, axis=-1, keepdims=True))
                 probs[at, :] = prob
                 rounded = prob.astype(BF16)
                 probs_b[at, :] = rounded
@@ -232,7 +228,7 @@
 
     def ctx_copies(group):
         src = ctx_own if group == 0 else ctx_all.at[ctx_rows(group), head_cols]
-        targets = [sibling] + [{"col": lax.rem(c + 2 * i, n_col)} for i in range(1, n_col // 2)]
+        targets = [{"col": lax.rem(c + i, n_col)} for i in range(1, n_col)]
         return [
             send(src, ctx_all.at[ctx_rows(group), head_cols], ctx_ss.at[group, i], ctx_rs.at[group, head], to)
             for i, to in enumerate(targets)
@@ -240,21 +236,11 @@
 
     def ctx_block(half, h):
         block = ctx_all.at[ctx_rows(half), fixed_cols[h]]
-        return send(block, block, fwd_ss.at[half, h], ctx_rs.at[half, h], sibling)
-
-    def passes_on(h):
-        return jnp.logical_and(core == owner(h) % 2, c != owner(h))
-
-    def ctx_forward(half):
-        for h in range(heads):
-            @pl.when(passes_on(h))
-            def _(h=h):
-                ctx_block(half, h).wait_recv()
-                ctx_block(half, h).start()
+        return send(block, block, ctx_ss.at[0, 0], ctx_rs.at[half, h], right)
 
     def ctx_wait(half):
         for h in range(heads):
-            @pl.when(core != owner(h) % 2)
+            @pl.when(c != owner(h))
             def _(h=h):
                 ctx_block(half, h).wait_recv()
 
@@ -303,12 +289,6 @@
             for group in range(3):
                 for copy in ctx_copies(group):
                     copy.wait_send()
-        for group in range(3):
-            for h in range(heads):
-                @pl.when(passes_on(h))
-                def _(h=h, group=group):
-                    ctx_block(group, h).wait_send()
-
     drain.append(ctx_drain)
 
     inner = reach // 2
@@ -441,7 +421,7 @@
             copy = send(stage.at[step - 1, :, sub_cols[u]], landed.at[step - 1, :, sub_cols[u]],
                         rs_ss.at[way, step - 1, u], rs_rs.at[way, step - 1, u], right if way == 0 else left)
             copy.start()
-            drain.append(copy.wait_send)
+            (drain if step < 3 else late).append(copy.wait_send)
 
     def out_both(step):
         if step < reach:
@@ -484,7 +464,7 @@
         copy = send(dw_stage.at[way, step - 1], dw_recv.at[way, step - 1], dw_ss.at[way, step - 1],
                     dw_rs.at[way, step - 1], up if way == 0 else down)
         copy.start()
-        drain.append(copy.wait_send)
+        late.append(copy.wait_send)
 
     def backward():
         @pl.when(is_head)
@@ -519,7 +499,7 @@
             for i in range(1, n_col):
                 dqkv_copy(i).wait_send()
 
-    drain.append(dqkv_drain)
+    late.append(dqkv_drain)
 
     def weight_ends():
         for way in range(2):
@@ -542,7 +522,7 @@
             @pl.when(c != owner(h))
             def _(h=h):
                 block = dqkv_all.at[:, :, fixed_cols[h]]
-                send(block, block, dq_ss.at[0], dq_rs.at[h], sibling).wait_recv()
+                send(block, block, dq_ss.at[0], dq_rs.at[h], right).wait_recv()
         for t, ref in enumerate((dq_ref, dk_ref, dv_ref)):
             ref[0] = dqkv_all[t]
 
@@ -552,18 +532,16 @@
     grad_step(2)
     forward(n_blocks // 2, n_blocks)
     cross_start()
+    ctx_start()
     cross_relay()
-    ctx_start()
     cross_finish(0)
     grad_step(3)
     for copy in weight_copies:
         copy.wait()
     context_grads([0])
-    ctx_forward(0)
     grad_step(4)
     context_grads([1, 2])
     ctx_wait(0)
-    ctx_forward(1)
     grad_step(5)
     ctx_wait(1)
     ctx_in_order(middle - reach, middle + reach)
@@ -571,12 +549,11 @@
     out_both(1)
     weight_near(0, n_y // 2)
     grad_step(6)
+    project_middle()
     out_both(2)
-    project_middle()
-    near_sum()
     cross_finish(1)
     grad_step(7)
-    ctx_forward(2)
+    near_sum()
     weight_near(n_y // 2, n_y)
     out_both(3)
     grad_step(8)
@@ -589,6 +566,8 @@
     weight_both(2)
     backward()
     weight_both(3)
+    for wait in drain:
+        wait()
     out_step(0, reach, final=True)
     out_step(1, reach + 1, final=True)
     for given, held in tiles:
@@ -596,7 +575,7 @@
     weight_step(0, n_y, final=True)
     weight_step(1, n_y, final=True)
     dqkv_finish()
-    for wait in drain:
+    for wait in late:
         wait()
 
 
@@ -625,6 +604,7 @@
         heads, ring, reach, n_y = width // HEAD_DIM, HALVES * n_row, n_row // 2, n_depth // HALVES
         stripe = cols // n_depth
         vmem = pl.BlockSpec(memory_space=pltpu.VMEM)
+        anywhere = pl.BlockSpec(memory_space=pltpu.HBM)
         dma = pltpu.SemaphoreType.DMA
         hops, turns = max(reach, 1), max(n_y - 1, 1)
         scratch = [
@@ -654,10 +634,10 @@
             pltpu.VMEM((n_y, 256, width), F32),
             pltpu.VMEM((2, turns, stripe // 2, width), BF16),
             pltpu.VMEM((2, turns, stripe // 2, width), BF16),
-            dma((THIRDS * n_y,)),
+            dma((THIRDS * n_y,)), dma((THIRDS * n_y,)), dma((3,)),
             dma((heads,)), dma((n_col,)),
             dma((2, ring // 2, THIRDS)), dma((2, ring // 2, THIRDS)),
-            dma((3, n_col)), dma((3, heads)), dma((3, heads)), dma((2, 2, 2)), dma((2, 2, 2)),
+            dma((3, n_col)), dma((3, heads)), dma((2, 2, 2)), dma((2, 2, 2)),
             dma((3, heads)), dma((3, n_col)), dma((2 * reach,)), dma((n_row,)),
             dma((n_col,)), dma((heads,)),
             dma((2, hops, SUBS)), dma((2, hops, SUBS)),
@@ -672,14 +652,13 @@
                 jax.ShapeDtypeStruct(v.shape, BF16),
                 jax.ShapeDtypeStruct((stripe, width), F32),
             ),
-            in_specs=[vmem] * 4 + [pl.BlockSpec(memory_space=pl.ANY), vmem],
+            in_specs=[anywhere] * 3 + [vmem] + [anywhere] * 2,
             out_specs=(vmem,) * 5,
             scratch_shapes=scratch,
             compiler_params=pltpu.CompilerParams(
                 collective_id=0, has_side_effects=True, vmem_limit_bytes=VMEM_BYTES
             ),
         )(q, k, v, positions, weight, grad)
-        anywhere = pl.BlockSpec(memory_space=pltpu.HBM)
         *parts, weight_grad = pl.pallas_call(
             hand_over,
             out_shape=[jax.ShapeDtypeStruct(part.shape, part.dtype) for part in parts],

time: 98 us -> 96.4 us (0.984)
  the two profiles are of different devices: /device:TPU:36 before, /device:TPU:24 now
where the time goes in v4:
time: 96.4 us; the launch traced here: 95.7 us
  Pallas kernels  95 us (99%)
    pallas_call x1, Pallas kernels, local(): pl.pallas_call(functools.partial(kernel, n_row, n_col, n_depth), out_shap...  92.8 us
    pallas_call x1, Pallas kernels, local(): pl.pallas_call(hand_over, out_shape=[jax.ShapeDtypeStruct(part.shape, par...  2.22 us

profile of v4, /device:TPU:24, one launch (start us, length us, event | category | flops | bytes accessed | tf_op | source)
XLA Modules:
  0.0 95.7 jit_solution(2604214937487094019)
XLA Ops:
  0.6 92.8 %shard_map.101 = (bf16[1,64,1536]{2,1,0:T(8,128)(2,1)}, bf16[1,64,768]{2,1,0:T(8,128)(2,1)}, bf16[1,64,768]{2,1,0:T(8,128)(2,1)}, bf16[1,64,768]{2,1,0:T(8,128)(2,1)}, f32[192,768]{1,0:T(8,128)}) custom-call(bf16[1,64,768]{2,1,0:T(8,128)(2,1)} %q_ref.1, bf16[1,64,768]{2,1,0:T(8,128)(2,1)} %k_ref.1, bf16[1,64,768]{2,1,0:T(8,128)(2,1)} %v_ref.1, ...), custom_call_target="tpu_custom_call" | custom-call | tf_op jit(solution)/shard_map/pallas_call | solution.py:646
  93.5 2.2 %shard_map.102 = (bf16[1,64,1536]{2,1,0:T(8,128)(2,1)}, bf16[1,64,768]{2,1,0:T(8,128)(2,1)}, bf16[1,64,768]{2,1,0:T(8,128)(2,1)}, bf16[1,64,768]{2,1,0:T(8,128)(2,1)}, f32[192,768]{1,0:T(8,128)}) custom-call(bf16[1,64,1536]{2,1,0:T(8,128)(2,1)} %get-tuple-element.15.refs_0_, bf16[1,64,768]{2,1,0:T(8,128)(2,1)} %get-tuple-element.16.refs_1_, ...), custom_call_target="tpu_custom_call" | custom-call | tf_op jit(solution)/shard_map/pallas_call | solution.py:662

commit v5 on v4

--- a/solution.py
+++ b/solution.py
@@ -41,15 +41,26 @@
     heads = width // HEAD_DIM
     scale = HEAD_DIM ** (-0.5)
 
+    def wrap(place, size):
+        place = jnp.where(place < 0, place + size, place)
+        return jnp.where(place >= size, place - size, place)
+
+    def in_half(place):
+        half = jnp.where(place >= n_row, 1, 0)
+        return place - half * n_row, half
+
     def on_ring(place):
-        place = lax.rem(place + 2 * ring, ring)
-        return {"row": lax.rem(place, n_row), "depth": y * HALVES + lax.div(place, n_row)}
+        line, half = in_half(wrap(place, ring))
+        return (line, c, y * HALVES + half)
+
+    def on_col(place):
+        return (r, place, d)
 
     def on_y(place):
-        return {"depth": lax.rem(place + n_y, n_y) * HALVES + b}
+        return (r, c, wrap(place, n_y) * HALVES + b)
 
     def chunk_at(offset):
-        return lax.rem(z + offset + 2 * ring, ring)
+        return wrap(z + offset, ring)
 
     def owner(h):
         return (h * n_col) // heads
@@ -72,7 +83,7 @@
         )
 
     barrier = pltpu.get_barrier_semaphore()
-    peers = [{"col": lax.rem(c + i, n_col)} for i in range(1, n_col)]
+    peers = [on_col(wrap(c + i, n_col)) for i in range(1, n_col)]
     peers += [right, left, other, up]
     if n_y > 2:
         peers += [down]
@@ -111,8 +122,7 @@
         if step <= near[way] or u == 1:
             action()
             return
-        place = lax.rem(place + ring, ring)
-        line, half = lax.rem(place, n_row), lax.div(place, n_row)
+        line, half = in_half(wrap(place, ring))
         onward = far[way] - step
         crosses = line + onward >= n_row if way == 0 else line - onward < 0
         pl.when(jnp.logical_or(crosses, half == (0 if u == 0 else 1)))(action)
@@ -145,7 +155,7 @@
     own_span = pl.ds(pl.multiple_of(c * span, span), span)
     def heads_copy(h):
         return send(qkv_stage.at[:, :, fixed_cols[h]], qkv.at[:, own_span, :],
-                    qkv_ss.at[h], qkv_rs.at[c], {"col": owner(h)})
+                    qkv_ss.at[h], qkv_rs.at[c], on_col(owner(h)))
 
     for h in range(heads):
         @pl.when(c != owner(h))
@@ -167,11 +177,12 @@
 
     block_rows = min(128, length)
 
-    def forward(first, last):
-        @pl.when(is_head)
-        def _():
-            for i in range(first, last):
-                at = pl.ds(i * block_rows, block_rows)
+    def forward(phase):
+        @pl.when(is_head)
+        def _():
+            base = crossing_half(r, phase) * half_rows
+            for i in range(n_blocks // 2):
+                at = pl.ds(pl.multiple_of(base + i * block_rows, block_rows), block_rows)
                 logits = lax.dot_general(qkv[0, at, :], qkv[1], NT, preferred_element_type=F32)
                 visible = pos_ref[...].astype(F32) <= pos_col[at, 0:1]
                 logits = jnp.where(visible, logits * scale, -jnp.inf)
@@ -193,9 +204,9 @@
                 jnp.broadcast_to(pos_ref[...].astype(F32), (128, length))
             )
             for i in range(1, n_col):
-                src = lax.rem(c + i, n_col)
+                src = wrap(c + i, n_col)
                 place = qkv.at[:, pl.ds(pl.multiple_of(src * span, span), span), :]
-                send(place, place, qkv_ss.at[0], qkv_rs.at[src], {"col": src}).wait_recv()
+                send(place, place, qkv_ss.at[0], qkv_rs.at[src], on_col(src)).wait_recv()
 
     half_rows, quarter = length // 2, length // 4
 
@@ -204,12 +215,15 @@
             return pl.ds(pl.multiple_of(b * length, length), length)
         return crossing_rows(1 - b, r, group - 1)
 
+    def crossing_half(line, phase):
+        return jnp.where(line < reach, 1 - phase, phase)
+
     def crossing_rows(place, line, phase):
-        start = place * length + jnp.where(line < reach, 1 - phase, phase) * half_rows
+        start = place * length + crossing_half(line, phase) * half_rows
         return pl.ds(pl.multiple_of(start, half_rows), half_rows)
 
     def crossing_part(place, line, phase, way):
-        start = place * length + jnp.where(line < reach, 1 - phase, phase) * half_rows + way * quarter
+        start = place * length + crossing_half(line, phase) * half_rows + way * quarter
         return pl.ds(pl.multiple_of(start, quarter), quarter)
 
     def cross_copy(phase, way):
@@ -218,7 +232,8 @@
 
     def relay_copy(phase, way):
         origin = chunk_at(-1 if way == 0 else 1)
-        at = crossing_part(lax.div(origin, n_row), lax.rem(origin, n_row), phase, way)
+        line, half = in_half(origin)
+        at = crossing_part(half, line, phase, way)
         return send(relay.at[phase, way], ctx_all.at[at, head_cols],
                     cross_ss.at[1, phase, way], cross_rs.at[1, phase, way], far_right if way == 0 else far_left)
 
@@ -228,7 +243,7 @@
 
     def ctx_copies(group):
         src = ctx_own if group == 0 else ctx_all.at[ctx_rows(group), head_cols]
-        targets = [{"col": lax.rem(c + i, n_col)} for i in range(1, n_col)]
+        targets = [on_col(wrap(c + i, n_col)) for i in range(1, n_col)]
         return [
             send(src, ctx_all.at[ctx_rows(group), head_cols], ctx_ss.at[group, i], ctx_rs.at[group, head], to)
             for i, to in enumerate(targets)
@@ -244,12 +259,11 @@
             def _(h=h):
                 ctx_block(half, h).wait_recv()
 
-    def cross_start():
-        @pl.when(is_head)
-        def _():
-            for phase in range(2):
-                for way in range(2):
-                    cross_copy(phase, way).start()
+    def cross_start(phase):
+        @pl.when(is_head)
+        def _():
+            for way in range(2):
+                cross_copy(phase, way).start()
 
     def ctx_start():
         @pl.when(is_head)
@@ -258,13 +272,12 @@
                 copy.start()
             ctx_all[ctx_rows(0), head_cols] = ctx_own[...]
 
-    def cross_relay():
-        @pl.when(is_head)
-        def _():
-            for phase in range(2):
-                for way in range(2):
-                    cross_copy(phase, way).wait_recv()
-                    relay_copy(phase, way).start()
+    def cross_relay(phase):
+        @pl.when(is_head)
+        def _():
+            for way in range(2):
+                cross_copy(phase, way).wait_recv()
+                relay_copy(phase, way).start()
 
     def cross_finish(phase):
         @pl.when(is_head)
@@ -292,47 +305,40 @@
     drain.append(ctx_drain)
 
     inner = reach // 2
-    near_parts = [(reach - inner, 2 * inner), (0, reach - inner), (reach + inner, reach - inner)]
+    near_slots = [list(range(reach - inner, reach + inner)),
+                  list(range(reach - inner)) + list(range(reach + inner, 2 * reach))]
+    held_at = {slot: i for i, slot in enumerate(near_slots[0] + near_slots[1])}
+    near_parts = [(0, 2 * inner), (2 * inner, 2 * reach - 2 * inner)]
 
     def near_copy(part, h):
         at = pl.ds(near_parts[part][0] * rows, near_parts[part][1] * rows)
         return send(cg_stage.at[at, fixed_cols[h]], cg_recv.at[c, at, :],
-                    cg_ss.at[part, h], cg_rs.at[part, c], {"col": owner(h)})
-
-    def context_grads(parts):
-        parts = [part for part in parts if near_parts[part][1] > 0]
-        if not parts:
+                    cg_ss.at[part, h], cg_rs.at[part, c], on_col(owner(h)))
+
+    def context_grads(part):
+        first, count = near_parts[part]
+        if count == 0:
             return
-        tokens = []
-        for part in parts:
-            first, count = near_parts[part]
-            slots = grad_all[middle - reach + first:middle - reach + first + count]
-            tokens.append(slots.reshape(count * rows, cols))
-        tokens = tokens[0] if len(tokens) == 1 else jnp.concatenate(tokens, axis=0)
+        tokens = jnp.concatenate([grad_all[middle - reach + slot] for slot in near_slots[part]], axis=0)
         for i in range(heads // 2):
             two = pl.ds(i * 2 * HEAD_DIM, 2 * HEAD_DIM)
-            product = lax.dot_general(tokens, w_ref[two, :], NT, preferred_element_type=F32).astype(BF16)
-            done = 0
-            for part in parts:
-                first, count = near_parts[part]
-                cg_stage[first * rows:(first + count) * rows, two] = product[done:done + count * rows]
-                done += count * rows
+            product = lax.dot_general(tokens, w_ref[two, :], NT, preferred_element_type=F32)
+            cg_stage[first * rows:(first + count) * rows, two] = product.astype(BF16)
             for h in (2 * i, 2 * i + 1):
                 @pl.when(c != owner(h))
                 def _(h=h):
-                    for part in parts:
-                        near_copy(part, h).start()
+                    near_copy(part, h).start()
 
     def near_sum():
         @pl.when(is_head)
         def _():
             cg_recv[c] = cg_stage[:, head_cols]
             for i in range(1, n_col):
-                src = lax.rem(c + i, n_col)
+                src = wrap(c + i, n_col)
                 for part, (first, count) in enumerate(near_parts):
                     if count > 0:
                         block = cg_recv.at[src, pl.ds(first * rows, count * rows), :]
-                        send(block, block, cg_ss.at[part, 0], cg_rs.at[part, src], {"col": src}).wait_recv()
+                        send(block, block, cg_ss.at[part, 0], cg_rs.at[part, src], on_col(src)).wait_recv()
             for i in range(2 * reach):
                 at = pl.ds(i * rows, rows)
                 total = cg_recv[0, at, :].astype(F32)
@@ -342,7 +348,7 @@
             for i in range(2 * reach):
                 @pl.when(is_own(i))
                 def _(i=i):
-                    cg_own[near_rows(i), :] = cg_near[i * rows:(i + 1) * rows, :]
+                    cg_own[near_rows(i), :] = cg_near[held_at[i] * rows:(held_at[i] + 1) * rows, :]
 
                 @pl.when(jnp.logical_not(is_own(i)))
                 def _(i=i):
@@ -353,13 +359,13 @@
         return jnp.logical_and(block >= 0, block < n_row)
 
     def near_block(i):
-        return lax.rem(r + i - reach + n_row, n_row)
+        return wrap(r + i - reach, n_row)
 
     def near_rows(i):
         return pl.ds(pl.multiple_of(near_block(i) * rows, rows), rows)
 
     def near_cross(i):
-        return send(cg_near.at[pl.ds(i * rows, rows), :], cg_own.at[near_rows(i), :],
+        return send(cg_near.at[pl.ds(held_at[i] * rows, rows), :], cg_own.at[near_rows(i), :],
                     cgx_ss.at[i], cgx_rs.at[near_block(i)], other)
 
     def cross_wait():
@@ -446,11 +452,11 @@
             dw_sum[place] = weight_product(place, middle - reach, middle + reach)
 
     def weight_far(place):
-        place = lax.rem(place + 2 * n_y, n_y)
+        place = wrap(place, n_y)
         dw_sum[place] += weight_product(place, 0, middle - reach) + weight_product(place, middle + reach, ring)
 
     def weight_step(way, step, final=False):
-        place = lax.rem(y + (-step if way == 0 else step) + 2 * n_y, n_y)
+        place = wrap(wrap(y + (-step if way == 0 else step), n_y), n_y)
         own = slice(way * part, (way + 1) * part)
         total = dw_sum[place, pl.ds(pl.multiple_of(b * 64 + way * part, 32), part), :]
         if step > 1:
@@ -489,9 +495,9 @@
                 dqkv_all[t, :, head_cols] = dqkv_own[t, own_span, :]
 
     def dqkv_copy(i):
-        to = lax.rem(c + i, n_col)
+        to = wrap(c + i, n_col)
         return send(dqkv_own.at[:, pl.ds(pl.multiple_of(to * span, span), span), :],
-                    dqkv_all.at[:, :, head_cols], dq_ss.at[i], dq_rs.at[head], {"col": to})
+                    dqkv_all.at[:, :, head_cols], dq_ss.at[i], dq_rs.at[head], on_col(to))
 
     def dqkv_drain():
         @pl.when(is_head)
@@ -528,19 +534,21 @@
 
     grad_step(1)
     heads_arrive()
-    forward(0, n_blocks // 2)
+    forward(0)
+    cross_start(0)
     grad_step(2)
-    forward(n_blocks // 2, n_blocks)
-    cross_start()
+    forward(1)
+    cross_relay(0)
+    cross_start(1)
     ctx_start()
-    cross_relay()
+    cross_relay(1)
     cross_finish(0)
     grad_step(3)
     for copy in weight_copies:
         copy.wait()
-    context_grads([0])
+    context_grads(0)
     grad_step(4)
-    context_grads([1, 2])
+    context_grads(1)
     ctx_wait(0)
     grad_step(5)
     ctx_wait(1)
@@ -638,7 +646,7 @@
             dma((heads,)), dma((n_col,)),
             dma((2, ring // 2, THIRDS)), dma((2, ring // 2, THIRDS)),
             dma((3, n_col)), dma((3, heads)), dma((2, 2, 2)), dma((2, 2, 2)),
-            dma((3, heads)), dma((3, n_col)), dma((2 * reach,)), dma((n_row,)),
+            dma((2, heads)), dma((2, n_col)), dma((2 * reach,)), dma((n_row,)),
             dma((n_col,)), dma((heads,)),
             dma((2, hops, SUBS)), dma((2, hops, SUBS)),
             dma((2, turns)), dma((2, turns)),

time: 96.4 us -> 96.9 us (level)
  Pallas kernels: 95 us -> 96.1 us
    pallas_call x1, Pallas kernels: 92.8 us -> 93.9 us  [local(): pl.pallas_call(functools.partial(kernel, n_row, n_col, n_depth), out_shap...]
where the time goes in v5:
time: 96.9 us; the launch traced here: 96.7 us
  Pallas kernels  96.1 us (99%)
    pallas_call x1, Pallas kernels, local(): pl.pallas_call(functools.partial(kernel, n_row, n_col, n_depth), out_shap...  93.9 us
    pallas_call x1, Pallas kernels, local(): pl.pallas_call(hand_over, out_shape=[jax.ShapeDtypeStruct(part.shape, par...  2.22 us

profile of v5, /device:TPU:24, one launch (start us, length us, event | category | flops | bytes accessed | tf_op | source)
XLA Modules:
  0.0 96.7 jit_solution(10719740003207588854)
XLA Ops:
  0.6 93.9 %shard_map.101 = (bf16[1,64,1536]{2,1,0:T(8,128)(2,1)}, bf16[1,64,768]{2,1,0:T(8,128)(2,1)}, bf16[1,64,768]{2,1,0:T(8,128)(2,1)}, bf16[1,64,768]{2,1,0:T(8,128)(2,1)}, f32[192,768]{1,0:T(8,128)}) custom-call(bf16[1,64,768]{2,1,0:T(8,128)(2,1)} %q_ref.1, bf16[1,64,768]{2,1,0:T(8,128)(2,1)} %k_ref.1, bf16[1,64,768]{2,1,0:T(8,128)(2,1)} %v_ref.1, ...), custom_call_target="tpu_custom_call" | custom-call | tf_op jit(solution)/shard_map/pallas_call | solution.py:654
  94.5 2.2 %shard_map.102 = (bf16[1,64,1536]{2,1,0:T(8,128)(2,1)}, bf16[1,64,768]{2,1,0:T(8,128)(2,1)}, bf16[1,64,768]{2,1,0:T(8,128)(2,1)}, bf16[1,64,768]{2,1,0:T(8,128)(2,1)}, f32[192,768]{1,0:T(8,128)}) custom-call(bf16[1,64,1536]{2,1,0:T(8,128)(2,1)} %get-tuple-element.15.refs_0_, bf16[1,64,768]{2,1,0:T(8,128)(2,1)} %get-tuple-element.16.refs_1_, ...), custom_call_target="tpu_custom_call" | custom-call | tf_op jit(solution)/shard_map/pallas_call | solution.py:670

commit v6 on v5

--- a/solution.py
+++ b/solution.py
@@ -9,7 +9,7 @@
 
 HEAD_DIM = 128
 HALVES = 2
-THIRDS = 3
+PARTS = 2
 SUBS = 2
 LANES = 128
 VMEM_BYTES = 56 * 1024 * 1024
@@ -24,7 +24,7 @@
     n_row, n_col, n_depth,
     q_ref, k_ref, v_ref, pos_ref, w_hbm, g_ref,
     out_ref, dq_ref, dk_ref, dv_ref, dw_ref,
-    w_ref, qkv_stage, qkv, pos_col, probs, probs_b, dlogits, ctx_own, ctx_all, ctx_rel, relay, grad_all,
+    w_ref, w_mid, g_mid, qkv_stage, qkv, pos_col, probs, probs_b, dlogits, ctx_own, ctx_all, ctx_rel, relay, grad_all,
     cg_stage, cg_recv, cg_near, cg_own, dqkv_own, dqkv_all,
     lo, rs_stage_r, rs_stage_l, rs_r, rs_l, dw_sum, dw_stage, dw_recv,
     w_sem, g_sem, in_sem, qkv_ss, qkv_rs, ag_ss, ag_rs, ctx_ss, ctx_rs, cross_ss, cross_rs, cg_ss, cg_rs, cgx_ss, cgx_rs, dq_ss, dq_rs,
@@ -91,47 +91,69 @@
         peers += [far_right, far_left]
     for peer in peers:
         pl.semaphore_signal(barrier, inc=1, device_id=peer, device_id_type=MESH)
-    third = cols // THIRDS
-    tiles = [(pl.ds((n * THIRDS + t) * LANES, LANES), pl.ds(t * third + n * LANES, LANES))
-             for n in range(n_y) for t in range(THIRDS)]
+    part_cols = cols // PARTS
+    lines = n_y * LANES
+    whole = [(pl.ds((n * 3 + 2 * u) * LANES, LANES), pl.ds(u * part_cols + n * LANES, LANES))
+             for n in range(n_y) for u in range(PARTS)]
+    middles = [pl.ds((n * 3 + 1) * LANES, LANES) for n in range(n_y)]
+
+    def middle_at(u, n):
+        return pl.ds(u * part_cols + lines + (n // 2) * LANES, LANES)
+
+    def swap_middles(first, second):
+        lower = lax.broadcasted_iota(jnp.int32, first.shape, 1) < LANES // 2
+        return (jnp.where(lower, first, pltpu.roll(second, LANES // 2, 1)),
+                jnp.where(lower, pltpu.roll(first, LANES // 2, 1), second))
+
+    def place_middles(staged, held):
+        for n in range(0, n_y, 2):
+            pair = [staged[:, (n + i) * LANES:(n + i + 1) * LANES].astype(F32) for i in range(2)]
+            for u, tile_values in enumerate(swap_middles(*pair)):
+                held[:, middle_at(u, n)] = tile_values.astype(BF16)
+
     weight_copies = [pltpu.make_async_copy(w_hbm.at[:, given], w_ref.at[:, held], w_sem.at[i])
-                     for i, (given, held) in enumerate(tiles)]
+                     for i, (given, held) in enumerate(whole)]
+    weight_copies += [pltpu.make_async_copy(w_hbm.at[:, given], w_mid.at[:, pl.ds(n * LANES, LANES)], w_sem.at[2 * n_y + n])
+                      for n, given in enumerate(middles)]
     head_copies = [pltpu.make_async_copy(ref.at[0], qkv_stage.at[t], in_sem.at[t])
                    for t, ref in enumerate((q_ref, k_ref, v_ref))]
     grad_copies = [pltpu.make_async_copy(g_ref.at[0, :, given], grad_all.at[middle, :, held], g_sem.at[i])
-                   for i, (given, held) in enumerate(tiles)]
+                   for i, (given, held) in enumerate(whole)]
+    grad_copies += [pltpu.make_async_copy(g_ref.at[0, :, given], g_mid.at[:, pl.ds(n * LANES, LANES)], g_sem.at[2 * n_y + n])
+                    for n, given in enumerate(middles)]
     for copy in grad_copies + head_copies + weight_copies:
         copy.start()
     for copy in grad_copies + head_copies:
         copy.wait()
+    place_middles(g_mid, grad_all.at[middle])
     pl.semaphore_wait(barrier, len(peers))
 
     drain, late = [], []
 
     far = [ring // 2, ring // 2 - 1]
     near = [reach, reach - 1]
-    third_cols = [pl.ds(u * third, third) for u in range(THIRDS)]
+    held_cols = [pl.ds(u * part_cols, part_cols) for u in range(PARTS)]
 
     def grad_copy(way, step, u):
         sign = -1 if way == 0 else 1
-        return send(grad_all.at[middle + sign * (step - 1), :, third_cols[u]],
-                    grad_all.at[middle + sign * step, :, third_cols[u]],
+        return send(grad_all.at[middle + sign * (step - 1), :, held_cols[u]],
+                    grad_all.at[middle + sign * step, :, held_cols[u]],
                     ag_ss.at[way, step - 1, u], ag_rs.at[way, step - 1, u], right if way == 0 else left)
 
     def where_needed(place, way, step, u, action):
-        if step <= near[way] or u == 1:
+        if step <= near[way]:
             action()
             return
         line, half = in_half(wrap(place, ring))
         onward = far[way] - step
         crosses = line + onward >= n_row if way == 0 else line - onward < 0
-        pl.when(jnp.logical_or(crosses, half == (0 if u == 0 else 1)))(action)
+        pl.when(jnp.logical_or(crosses, half == u))(action)
 
     def grad_start(way, step, u):
         where_needed(z + (1 if way == 0 else -1), way, step, u, grad_copy(way, step, u).start)
 
     def grad_step(step):
-        for u in (1, 0, 2):
+        for u in range(PARTS):
             for way in range(2):
                 if step <= far[way]:
                     def pass_on(way=way, u=u):
@@ -144,11 +166,11 @@
     def grad_drain():
         for way in range(2):
             for step in range(1, far[way] + 1):
-                for u in range(THIRDS):
+                for u in range(PARTS):
                     where_needed(z + (1 if way == 0 else -1), way, step, u, grad_copy(way, step, u).wait_send)
 
     drain.append(grad_drain)
-    for u in (1, 0, 2):
+    for u in range(PARTS):
         for way in range(2):
             grad_start(way, 1, u)
 
@@ -439,10 +461,8 @@
     part = stripe // 2
 
     def weight_product(place, first, last):
-        pair = [
-            grad_all[first:last, :, pl.ds(pl.multiple_of((b + i) * third + place * LANES, LANES), LANES)]
-            for i in range(2)
-        ]
+        starts = (b * part_cols + place * LANES, b * part_cols + lines + lax.div(place, 2) * LANES)
+        pair = [grad_all[first:last, :, pl.ds(pl.multiple_of(start, LANES), LANES)] for start in starts]
         tokens = jnp.concatenate(pair, axis=-1).reshape((last - first) * rows, 2 * LANES)
         return lax.dot_general(tokens, ctx_rel[first * rows:last * rows, :], TN, preferred_element_type=F32)
 
@@ -457,14 +477,22 @@
 
     def weight_step(way, step, final=False):
         place = wrap(wrap(y + (-step if way == 0 else step), n_y), n_y)
-        own = slice(way * part, (way + 1) * part)
-        total = dw_sum[place, pl.ds(pl.multiple_of(b * 64 + way * part, 32), part), :]
+        if way == 0:
+            total = dw_sum[place, 0:part, :]
+        else:
+            shared = pl.ds(pl.multiple_of(LANES + lax.rem(place, 2) * (LANES // 2), LANES // 2), LANES // 2)
+            total = jnp.concatenate([dw_sum[place, part:LANES, :], dw_sum[place, shared, :]], axis=0)
         if step > 1:
             block = dw_recv.at[way, step - 2]
             send(block, block, dw_ss.at[way, step - 2], dw_rs.at[way, step - 2], up).wait_recv()
             total = total + block[...].astype(F32)
         if final:
-            dw_ref[own, :] = total
+            tile_start = b * (LANES // 2)
+            if way == 0:
+                dw_ref[pl.ds(pl.multiple_of(tile_start, LANES // 2), part), :] = total
+            else:
+                dw_ref[pl.ds(pl.multiple_of(tile_start + part, 32), LANES - part), :] = total[:LANES - part]
+                dw_ref[pl.ds(pl.multiple_of((1 - b) * LANES, LANES), LANES // 2), :] = total[LANES - part:]
             return
         dw_stage[way, step - 1] = total.astype(BF16)
         copy = send(dw_stage.at[way, step - 1], dw_recv.at[way, step - 1], dw_ss.at[way, step - 1],
@@ -546,6 +574,7 @@
     grad_step(3)
     for copy in weight_copies:
         copy.wait()
+    place_middles(w_mid, w_ref)
     context_grads(0)
     grad_step(4)
     context_grads(1)
@@ -578,8 +607,12 @@
         wait()
     out_step(0, reach, final=True)
     out_step(1, reach + 1, final=True)
-    for given, held in tiles:
+    for given, held in whole:
         out_ref[0, :, given] = lo[reach, :, held].astype(BF16)
+    for n in range(0, n_y, 2):
+        pair = swap_middles(lo[reach, :, middle_at(0, n)], lo[reach, :, middle_at(1, n)])
+        for i in range(2):
+            out_ref[0, :, middles[n + i]] = pair[i].astype(BF16)
     weight_step(0, n_y, final=True)
     weight_step(1, n_y, final=True)
     dqkv_finish()
@@ -617,6 +650,8 @@
         hops, turns = max(reach, 1), max(n_y - 1, 1)
         scratch = [
             pltpu.VMEM((width, cols), BF16),
+            pltpu.VMEM((width, n_y * LANES), BF16),
+            pltpu.VMEM((rows, n_y * LANES), BF16),
             pltpu.VMEM((3, span, width), BF16),
             pltpu.VMEM((3, length, HEAD_DIM), BF16),
             pltpu.VMEM((length, 128), F32),
@@ -642,9 +677,9 @@
             pltpu.VMEM((n_y, 256, width), F32),
             pltpu.VMEM((2, turns, stripe // 2, width), BF16),
             pltpu.VMEM((2, turns, stripe // 2, width), BF16),
-            dma((THIRDS * n_y,)), dma((THIRDS * n_y,)), dma((3,)),
+            dma((3 * n_y,)), dma((3 * n_y,)), dma((3,)),
             dma((heads,)), dma((n_col,)),
-            dma((2, ring // 2, THIRDS)), dma((2, ring // 2, THIRDS)),
+            dma((2, ring // 2, PARTS)), dma((2, ring // 2, PARTS)),
             dma((3, n_col)), dma((3, heads)), dma((2, 2, 2)), dma((2, 2, 2)),
             dma((2, heads)), dma((2, n_col)), dma((2 * reach,)), dma((n_row,)),
             dma((n_col,)), dma((heads,)),

time: 96.9 us -> 93.8 us (0.968)
  Pallas kernels: 96.1 us -> 92.3 us
    pallas_call x1, Pallas kernels: 93.9 us -> 90.1 us  [local(): pl.pallas_call(functools.partial(kernel, n_row, n_col, n_depth), out_shap...]
where the time goes in v6:
time: 93.8 us; the launch traced here: 93 us
  Pallas kernels  92.3 us (98%)
    pallas_call x1, Pallas kernels, local(): pl.pallas_call(functools.partial(kernel, n_row, n_col, n_depth), out_shap...  90.1 us
    pallas_call x1, Pallas kernels, local(): pl.pallas_call(hand_over, out_shape=[jax.ShapeDtypeStruct(part.shape, par...  2.22 us

profile of v6, /device:TPU:24, one launch (start us, length us, event | category | flops | bytes accessed | tf_op | source)
XLA Modules:
  0.0 93.0 jit_solution(15699631908098851057)
XLA Ops:
  0.6 90.1 %shard_map.101 = (bf16[1,64,1536]{2,1,0:T(8,128)(2,1)}, bf16[1,64,768]{2,1,0:T(8,128)(2,1)}, bf16[1,64,768]{2,1,0:T(8,128)(2,1)}, bf16[1,64,768]{2,1,0:T(8,128)(2,1)}, f32[192,768]{1,0:T(8,128)}) custom-call(bf16[1,64,768]{2,1,0:T(8,128)(2,1)} %q_ref.1, bf16[1,64,768]{2,1,0:T(8,128)(2,1)} %k_ref.1, bf16[1,64,768]{2,1,0:T(8,128)(2,1)} %v_ref.1, ...), custom_call_target="tpu_custom_call" | custom-call | tf_op jit(solution)/shard_map/pallas_call | solution.py:689
  90.8 2.2 %shard_map.102 = (bf16[1,64,1536]{2,1,0:T(8,128)(2,1)}, bf16[1,64,768]{2,1,0:T(8,128)(2,1)}, bf16[1,64,768]{2,1,0:T(8,128)(2,1)}, bf16[1,64,768]{2,1,0:T(8,128)(2,1)}, f32[192,768]{1,0:T(8,128)}) custom-call(bf16[1,64,1536]{2,1,0:T(8,128)(2,1)} %get-tuple-element.15.refs_0_, bf16[1,64,768]{2,1,0:T(8,128)(2,1)} %get-tuple-element.16.refs_1_, ...), custom_call_target="tpu_custom_call" | custom-call | tf_op jit(solution)/shard_map/pallas_call | solution.py:705

commit v7 on v6

--- a/solution.py
+++ b/solution.py
@@ -123,7 +123,7 @@
                     for n, given in enumerate(middles)]
     for copy in grad_copies + head_copies + weight_copies:
         copy.start()
-    for copy in grad_copies + head_copies:
+    for copy in grad_copies:
         copy.wait()
     place_middles(g_mid, grad_all.at[middle])
     pl.semaphore_wait(barrier, len(peers))
@@ -175,6 +175,8 @@
             grad_start(way, 1, u)
 
     own_span = pl.ds(pl.multiple_of(c * span, span), span)
+    for copy in head_copies:
+        copy.wait()
     def heads_copy(h):
         return send(qkv_stage.at[:, :, fixed_cols[h]], qkv.at[:, own_span, :],
                     qkv_ss.at[h], qkv_rs.at[c], on_col(owner(h)))
@@ -584,17 +586,16 @@
     ctx_in_order(middle - reach, middle + reach)
     project_ends()
     out_both(1)
-    weight_near(0, n_y // 2)
     grad_step(6)
     project_middle()
     out_both(2)
     cross_finish(1)
     grad_step(7)
     near_sum()
-    weight_near(n_y // 2, n_y)
+    weight_near(0, n_y)
     out_both(3)
+    ctx_wait(2)
     grad_step(8)
-    ctx_wait(2)
     ctx_in_order(0, middle - reach)
     ctx_in_order(middle + reach, ring)
     weight_ends()

time: 93.8 us -> 94.7 us (level)
  no operation moved by 1% of the time
where the time goes in v7:
time: 94.7 us; the launch traced here: 93.6 us
  Pallas kernels  93 us (98%)
    pallas_call x1, Pallas kernels, local(): pl.pallas_call(functools.partial(kernel, n_row, n_col, n_depth), out_shap...  90.8 us
    pallas_call x1, Pallas kernels, local(): pl.pallas_call(hand_over, out_shape=[jax.ShapeDtypeStruct(part.shape, par...  2.22 us

profile of v7, /device:TPU:24, one launch (start us, length us, event | category | flops | bytes accessed | tf_op | source)
XLA Modules:
  0.0 93.6 jit_solution(16811779712275404821)
XLA Ops:
  0.6 90.8 %shard_map.101 = (bf16[1,64,1536]{2,1,0:T(8,128)(2,1)}, bf16[1,64,768]{2,1,0:T(8,128)(2,1)}, bf16[1,64,768]{2,1,0:T(8,128)(2,1)}, bf16[1,64,768]{2,1,0:T(8,128)(2,1)}, f32[192,768]{1,0:T(8,128)}) custom-call(bf16[1,64,768]{2,1,0:T(8,128)(2,1)} %q_ref.1, bf16[1,64,768]{2,1,0:T(8,128)(2,1)} %k_ref.1, bf16[1,64,768]{2,1,0:T(8,128)(2,1)} %v_ref.1, ...), custom_call_target="tpu_custom_call" | custom-call | tf_op jit(solution)/shard_map/pallas_call | solution.py:690
  91.4 2.2 %shard_map.102 = (bf16[1,64,1536]{2,1,0:T(8,128)(2,1)}, bf16[1,64,768]{2,1,0:T(8,128)(2,1)}, bf16[1,64,768]{2,1,0:T(8,128)(2,1)}, bf16[1,64,768]{2,1,0:T(8,128)(2,1)}, f32[192,768]{1,0:T(8,128)}) custom-call(bf16[1,64,1536]{2,1,0:T(8,128)(2,1)} %get-tuple-element.15.refs_0_, bf16[1,64,768]{2,1,0:T(8,128)(2,1)} %get-tuple-element.16.refs_1_, ...), custom_call_target="tpu_custom_call" | custom-call | tf_op jit(solution)/shard_map/pallas_call | solution.py:706
